TPU v7x, 256 devices: a whole 4x4x8 slice. The times are simulated.
256 devices in a mesh: dp: 8 (over z), seq: 32 (over y, x, core).
Axes of the slice: x: 4, y: 4, z: 8, core: 2. Of those that a mesh axis runs over, the one named last changes fastest.
Arguments:
- tokens: bfloat16 [8, 16384, 1024], P('dp', 'seq'), may hold values from -6 to 6
- grad_out: bfloat16 [8, 16384, 1024], P('dp', 'seq'), may hold values from -6 to 6
- src_order: int32 [32, 32], P('seq'), may hold values from 0 to 31, each once within a row
- dst_order: int32 [32, 32], P('seq'), may hold values from 0 to 31, each once within a row
- w_proj: bfloat16 [1024, 1152], replicated, may hold values from -0.0234375 to 0.0234375
- w_dt: bfloat16 [1024, 16], replicated, may hold values from -0.1875 to 0.1875
- w_out: bfloat16 [1024, 1024], replicated, may hold values from -0.1875 to 0.1875
- dt_bias: float32 [16], replicated, may hold values from -0.5 to 1
- decay_rate: float32 [16], replicated, may hold values from 1.2207031e-05 to 0.04, as said below
- d_skip: float32 [16], replicated, may hold values from 0.5 to 2
- norm_gain: float32 [1024], replicated, may hold values from 0.5 to 1.5
Outputs:
- grad_tokens: bfloat16 [8, 16384, 1024], P('dp', 'seq')
- grad_w_proj: float32 [1024, 1152], P('seq')
- grad_w_dt: float32 [1024, 16], P('seq')
- grad_w_out: float32 [1024, 1024], P(None, 'seq')
Inputs may be any that keep to these rules, and one draw needn't show every extreme that they name: `src_order`: each row is a permutation of 0 to 31. `dst_order`: each row is a permutation of 0 to 31. `decay_rate`: positive rates.
All inputs are finite; a program needn't handle non-finite values.
Results may differ from a plain program's by a relative error of at most 0.005.
Values may be sent and summed in bfloat16 or wider, within the bound.
A program may use at most 192 MiB of HBM per device.

v0:
```python
from functools import partial

import jax
import jax.numpy as jnp
from jax import lax
from jax.sharding import PartitionSpec as P

H = 16
P_SIZE = 64
N = 64
SPAN = 256


HIGHEST = lax.Precision.HIGHEST
EPSILON = 1e-05


def passed_along(value, axis, by):
    peers = lax.axis_size(axis)
    pairs = [(i, i + by) for i in range(peers) if 0 <= i + by < peers]
    return lax.ppermute(value, axis, pairs)


def span_step(state, block):
    values, delta, decay_log, inject, readout = block
    running = jnp.cumsum(decay_log, axis=0)
    length = running.shape[0]
    lower = jnp.arange(length)[:, None] >= jnp.arange(length)[None, :]
    spread = running.T[:, :, None] - running.T[:, None, :]
    decay = jnp.exp(jnp.where(lower[None, :, :], spread, -jnp.inf))
    scores = jnp.dot(readout, inject.T, precision=HIGHEST)
    mixing = decay * scores[None, :, :] * delta.T[:, None, :]
    inside = jnp.einsum("hts,shp->thp", mixing, values, precision=HIGHEST)
    carried = (
        jnp.einsum("tn,hpn->thp", readout, state, precision=HIGHEST) * jnp.exp(running)[:, :, None]
    )
    total = running[-1]
    weight = jnp.exp(total[None, :] - running) * delta
    added = jnp.einsum("thp,tn->hpn", values * weight[:, :, None], inject, precision=HIGHEST)
    return (jnp.exp(total)[:, None, None] * state + added, inside + carried)


def ssd_scan(values, delta_raw, inject_read, start, dt_bias, decay_rate):
    count = values.shape[0]
    blocks = count // SPAN
    delta = jax.nn.softplus(delta_raw + dt_bias[None, :])
    decay_log = -decay_rate[None, :] * delta
    pieces = (
        values.reshape(blocks, SPAN, H, P_SIZE),
        delta.reshape(blocks, SPAN, H),
        decay_log.reshape(blocks, SPAN, H),
        inject_read[:, :N].reshape(blocks, SPAN, N),
        inject_read[:, N:].reshape(blocks, SPAN, N),
    )
    final, outputs = lax.scan(jax.checkpoint(span_step), start, pieces)
    return (outputs.reshape(count, H * P_SIZE), final)


def finish(mixed, values, d_skip, norm_gain):
    count = mixed.shape[0]
    summed = (mixed + jnp.repeat(d_skip, P_SIZE)[None, :] * values).reshape(count, H, P_SIZE)
    scale = lax.rsqrt(jnp.mean(summed * summed, axis=2, keepdims=True) + EPSILON)
    return (summed * scale).reshape(count, H * P_SIZE) * norm_gain[None, :]


def column_term(source, grads):
    return lax.dot_general(
        source, grads, (((0,), (0,)), ((), ())), preferred_element_type=jnp.float32
    )


def local(
    tokens,
    grad_out,
    src_order,
    dst_order,
    w_proj,
    w_dt,
    w_out,
    dt_bias,
    decay_rate,
    d_skip,
    norm_gain,
):
    seq_count = lax.axis_size("seq")
    clip_count = lax.axis_size("dp")
    count = tokens.shape[1]
    width = tokens.shape[2]
    inner = H * P_SIZE
    leaving = src_order[0]
    arrival = dst_order[0]
    block_count = leaving.shape[0]
    block = count // block_count

    def depart(array):
        grouped = jnp.take(array.reshape(block_count, block, width), leaving, axis=0)
        return grouped

    def settle(array):
        return jnp.take(array, arrival, axis=0).reshape(count, width)

    moved_tokens, moved_grads = (
        lax.all_to_all(depart(tokens[0]), "seq", split_axis=0, concat_axis=0, tiled=True),
        lax.all_to_all(depart(grad_out[0]), "seq", split_axis=0, concat_axis=0, tiled=True),
    )
    scan_tokens = settle(moved_tokens)
    scan_grads = settle(moved_grads)
    projected = jnp.dot(scan_tokens, w_proj, preferred_element_type=jnp.float32)
    delta_raw = jnp.dot(scan_tokens, w_dt, preferred_element_type=jnp.float32)
    values = projected[:, :inner]
    inject_read = projected[:, inner:]
    delta = jax.nn.softplus(delta_raw + dt_bias[None, :])
    running = jnp.cumsum(-decay_rate[None, :] * delta, axis=0)
    total = running[-1]
    keep = jnp.exp(total)
    weight = jnp.exp(total[None, :] - running) * delta
    local_state = jnp.einsum(
        "thp,tn->hpn",
        values.reshape(count, H, P_SIZE) * weight[:, :, None],
        inject_read[:, :N],
        precision=HIGHEST,
    )
    zero_state = jnp.zeros_like(local_state)

    def relay_state(turn, passing):
        return passed_along(keep[:, None, None] * passing + local_state, "seq", 1)

    entering = lax.fori_loop(0, seq_count - 1, relay_state, zero_state)
    (mixed, final), ssd_back = jax.vjp(
        partial(ssd_scan, dt_bias=dt_bias, decay_rate=decay_rate),
        values,
        delta_raw,
        inject_read,
        entering,
    )
    normed, finish_back = jax.vjp(
        partial(finish, d_skip=d_skip, norm_gain=norm_gain), mixed, values
    )
    grad_normed = jnp.dot(scan_grads, w_out.T, preferred_element_type=jnp.float32)
    grad_mixed, grad_skip = finish_back(grad_normed)
    outgoing = jnp.einsum(
        "thp,tn->hpn",
        grad_mixed.reshape(count, H, P_SIZE) * jnp.exp(running)[:, :, None],
        inject_read[:, N:],
        precision=HIGHEST,
    )

    def relay_grad(turn, passing):
        return passed_along(outgoing + keep[:, None, None] * passing, "seq", -1)

    leaving_grad = lax.fori_loop(0, seq_count - 1, relay_grad, zero_state)
    grad_values, grad_delta, grad_inject, unused = ssd_back((grad_mixed, leaving_grad))
    grad_proj = jnp.concatenate([grad_values + grad_skip, grad_inject], axis=1).astype(jnp.bfloat16)
    grad_delta_low = grad_delta.astype(jnp.bfloat16)
    grad_scan = (
        jnp.dot(grad_proj, w_proj.T, preferred_element_type=jnp.float32)
        + jnp.dot(grad_delta_low, w_dt.T, preferred_element_type=jnp.float32)
    ).astype(jnp.bfloat16)
    inverse_arrival = jnp.argsort(arrival)
    inverse_leaving = jnp.argsort(leaving)
    returning = jnp.take(grad_scan.reshape(block_count, block, width), inverse_arrival, axis=0)
    received = lax.all_to_all(returning, "seq", split_axis=0, concat_axis=0, tiled=True)
    grad_tokens = jnp.take(received, inverse_leaving, axis=0)
    grad_tokens = grad_tokens.reshape(1, count, width)
    normed_low = normed.astype(jnp.bfloat16)
    out_term = lax.dot_general(
        normed_low, scan_grads, (((0,), (0,)), ((), ())), preferred_element_type=jnp.float32
    )
    delta_term = lax.dot_general(
        scan_tokens, grad_delta_low, (((0,), (0,)), ((), ())), preferred_element_type=jnp.float32
    )
    out_part, delta_part = (
        lax.psum_scatter(out_term, "seq", scatter_dimension=1, tiled=True),
        lax.psum_scatter(delta_term, "seq", scatter_dimension=0, tiled=True),
    )
    proj_part = lax.psum_scatter(
        column_term(scan_tokens, grad_proj), "seq", scatter_dimension=0, tiled=True
    )
    proj_part, out_part, delta_part = lax.psum((proj_part, out_part, delta_part), "dp")
    scale = (clip_count * seq_count * count) ** (-0.5)
    return (grad_tokens, proj_part * scale, delta_part * scale, out_part * scale)


def solution(mesh):
    in_specs = (
        P("dp", "seq", None),
        P("dp", "seq", None),
        P("seq", None),
        P("seq", None),
        P(),
        P(),
        P(),
        P(),
        P(),
        P(),
        P(),
    )
    out_specs = (P("dp", "seq", None), P("seq", None), P("seq", None), P(None, "seq"))
    return jax.shard_map(local, mesh=mesh, in_specs=in_specs, out_specs=out_specs, check_vma=False)
```

profile of v0, /device:TPU:24, one launch (start us, length us, event | category | flops | bytes accessed | tf_op | source)
XLA Modules:
  0.0 1536.7 jit_solution(93001202305015782)
XLA Ops:
  15.8 22.5 %all_to_all.15 = bf16[32,16,1024]{2,1,0:T(8,128)(2,1)} all-to-all(bf16[32,16,1024]{2,1,0:T(8,128)(2,1)S(1)} %get-tuple-element.703), channel_id=1, replica_groups=mesh['dp'=8,'seq'=32] {'seq'}, dimensions={0} | all-to-all | bytes 2097152 | tf_op jit(solution)/shard_map/all_to_all | solution.py:104
  48.8 10.8 all-to-all-done
  85.8 425.5 %while.60 = (s32[]{:T(128)}, f32[16,64,64]{2,1,0:T(8,128)S(1)}, f32[16]{0:T(128)S(1)}, f32[16,64,64]{2,1,0:T(8,128)S(1)}, s32[]{:T(128)}) while((s32[]{:T(128)}, f32[16,64,64]{2,1,0:T(8,128)S(1)}, f32[16]{0:T(128)S(1)}, f32[16,64,64]{2,1,0:T(8,128)S(1)}, s32[]{:T(128)}) %tuple.143), condition=%wide.region_3.5_spmd, body=%wide.region_2.4_spmd.sunk | while | flops 131074 | bytes 1835173 | solution.py:128
  88.8 10.8 collective-permute-done
  102.4 10.9 collective-permute-done
  116.1 10.9 collective-permute-done
  129.9 10.9 collective-permute-done
  143.6 10.9 collective-permute-done
  157.3 10.9 collective-permute-done
  171.0 10.9 collective-permute-done
  184.8 10.9 collective-permute-done
  198.5 10.9 collective-permute-done
  212.2 10.9 collective-permute-done
  225.9 10.9 collective-permute-done
  239.7 10.9 collective-permute-done
  253.4 10.9 collective-permute-done
  267.1 10.9 collective-permute-done
  280.8 10.9 collective-permute-done
  294.6 10.9 collective-permute-done
  308.3 10.9 collective-permute-done
  322.0 10.9 collective-permute-done
  335.7 10.9 collective-permute-done
  349.5 10.9 collective-permute-done
  363.2 10.9 collective-permute-done
  376.9 10.9 collective-permute-done
  390.6 10.9 collective-permute-done
  404.3 10.9 collective-permute-done
  418.1 10.9 collective-permute-done
  431.8 10.9 collective-permute-done
  445.5 10.9 collective-permute-done
  459.2 10.9 collective-permute-done
  473.0 10.9 collective-permute-done
  486.7 10.9 collective-permute-done
  500.4 10.9 collective-permute-done
  512.9 22.4 %while.63 = (s32[]{:T(128)}, f32[16,64,64]{2,1,0:T(8,128)S(1)}, f32[2,256,16,64]{1,3,2,0:T(8,128)}, f32[2,16,64,64]{3,2,1,0:T(8,128)}, f32[2,256,16]{1,2,0:T(8,1...) while((s32[]{:T(128)}, f32[16,64,64]{2,1,0:T(8,128)S(1)}, ...), condition=%wide.region_7.9_spmd.clone, body=%wide.region_4.8_spmd.clone.sunk | while | flops 1263939584 | bytes 33690728 | solution.py:55
  579.0 426.1 %while.61 = (s32[]{:T(128)}, f32[16,64,64]{2,1,0:T(8,128)}, f32[16]{0:T(128)S(1)}, f32[16,64,64]{2,1,0:T(8,128)S(1)}, s32[]{:T(128)}) while((s32[]{:T(128)}, f32[16,64,64]{2,1,0:T(8,128)}, f32[16]{0:T(128)S(1)}, f32[16,64,64]{2,1,0:T(8,128)S(1)}, s32[]{:T(128)}) %tuple.170), condition=%wide.region_11.13_spmd, body=%wide.region_10.12_spmd.sunk | while | flops 131074 | bytes 1835173 | solution.py:151
  582.1 6.7 collective-permute-done.1
  596.0 6.7 collective-permute-done.1
  609.9 6.7 collective-permute-done.1
  623.7 6.7 collective-permute-done.1
  637.6 6.7 collective-permute-done.1
  651.5 6.7 collective-permute-done.1
  665.4 6.7 collective-permute-done.1
  679.2 6.7 collective-permute-done.1
  693.1 6.7 collective-permute-done.1
  707.0 6.7 collective-permute-done.1
  720.9 6.7 collective-permute-done.1
  734.8 6.7 collective-permute-done.1
  748.6 6.7 collective-permute-done.1
  762.5 6.7 collective-permute-done.1
  776.4 6.7 collective-permute-done.1
  831.9 6.7 collective-permute-done.1
  845.8 6.7 collective-permute-done.1
  956.8 6.7 collective-permute-done.1
  970.7 6.7 collective-permute-done.1
  1009.4 152.0 %while.62 = (s32[]{:T(128)}, f32[16,64,64]{2,1,0:T(8,128)}, f32[2,256,16,64]{1,3,2,0:T(8,128)}, f32[2,256,16]{2,1,0:T(8,128)}, f32[2,256,16]{1,0,2:T(2,128)}, /*...) while((s32[]{:T(128)}, f32[16,64,64]{2,1,0:T(8,128)}, ...), condition=%wide.region_25.27_spmd, body=%wide.region_12.26_spmd.sunk | while | flops 2789810176 | bytes 42585964 | solution.py:55
  1025.4 8.3 fusion.219
  1101.2 8.3 fusion.219
  1216.3 8.3 all-to-all-start.2
  1226.3 37.4 %reduce-scatter.10.cloned.1.call-done = f32[32,16]{1,0:T(8,128)} async-done(((f32[1024,16]{1,0:T(8,128)}), f32[32,16]{1,0:T(8,128)}) %reduce-scatter.10.cloned.1.call-update) | async-done | bytes 2064
  1264.5 17.7 %psum.22 = f32[32,16]{0,1:T(8,128)S(1)} all-reduce(f32[32,16]{0,1:T(8,128)S(1)} %copy.288), channel_id=1, replica_groups=mesh['dp'=8,'seq'=32] {'dp'}, use_global_device_ids=true, to_apply=%region_31.33 | all-reduce | flops 512 | bytes 4096 | tf_op jit(solution)/shard_map/psum | solution.py:179
  1282.2 74.4 %reduce-scatter.8.cloned.1.call-done = f32[1024,32]{0,1:T(8,128)} async-done(((f32[1024,1024]{0,1:T(8,128)}), f32[1024,32]{0,1:T(8,128)}) %reduce-scatter.8.cloned.1.call-update) | async-done | bytes 131088 | tf_op jit(solution)/shard_map/reduce_scatter | solution.py:173
  1356.7 95.2 %reduce-scatter.6.cloned.1.call-done = f32[32,1152]{1,0:T(8,128)} async-done(((f32[1024,1152]{1,0:T(8,128)}), f32[32,1152]{1,0:T(8,128)}) %reduce-scatter.6.cloned.1.call-update) | async-done | bytes 147472 | tf_op jit(solution)/shard_map/reduce_scatter | solution.py:176
  1455.5 71.3 %all-reduce.6.cloned.1.call-done = (f32[32,1152]{1,0:T(8,128)}, f32[1024,32]{0,1:T(8,128)}) async-done(((f32[32,1152]{1,0:T(8,128)}, f32[1024,32]{0,1:T(8,128)}), (f32[32,1152]{1,0:T(8,128)}, f32[1024,32]{0,1:T(8,128)})) %all-reduce.6.cloned.1.call-update) | async-done | bytes 278544 | tf_op jit(solution)/shard_map/psum | solution.py:179
  (511 shorter events, 701.7 us)
Async XLA Ops:
  38.3 21.3 %all-to-all-start = ((bf16[32,16,1024]{2,1,0:T(8,128)(2,1)}), bf16[32,16,1024]{2,1,0:T(8,128)(2,1)S(1)}, u32[]{:S(2)}, u32[]{:S(2)}) async-start(bf16[32,16,1024]{2,1,0:T(8,128)(2,1)} %get-tuple-element.704), calls=%async_computation | async-start | bytes 2097152 | tf_op jit(solution)/shard_map/all_to_all | solution.py:103
  44.4 1219.3 %reduce-scatter.10.cloned.1.call-start = ((), (), s32[]{:S(2)}) async-start(), calls=%async_computation.8 | async-start | bytes 540672
  86.8 12.8 collective-permute-start
  100.5 12.8 collective-permute-start
  114.2 12.8 collective-permute-start
  127.9 12.8 collective-permute-start
  141.7 12.8 collective-permute-start
  155.4 12.8 collective-permute-start
  169.1 12.8 collective-permute-start
  182.8 12.8 collective-permute-start
  196.6 12.8 collective-permute-start
  210.3 12.8 collective-permute-start
  224.0 12.8 collective-permute-start
  237.7 12.8 collective-permute-start
  251.5 12.8 collective-permute-start
  265.2 12.8 collective-permute-start
  278.9 12.8 collective-permute-start
  292.6 12.8 collective-permute-start
  306.4 12.8 collective-permute-start
  320.1 12.8 collective-permute-start
  333.8 12.8 collective-permute-start
  347.5 12.8 collective-permute-start
  361.3 12.8 collective-permute-start
  375.0 12.8 collective-permute-start
  388.7 12.8 collective-permute-start
  402.4 12.8 collective-permute-start
  416.2 12.8 collective-permute-start
  429.9 12.8 collective-permute-start
  443.6 12.8 collective-permute-start
  457.3 12.8 collective-permute-start
  471.0 12.8 collective-permute-start
  484.8 12.8 collective-permute-start
  498.5 12.8 collective-permute-start
  589.9 12.7 collective-permute-start.1
  603.8 12.7 collective-permute-start.1
  617.7 12.7 collective-permute-start.1
  631.6 12.7 collective-permute-start.1
  645.4 12.7 collective-permute-start.1
  659.3 12.7 collective-permute-start.1
  673.2 12.7 collective-permute-start.1
  687.1 12.7 collective-permute-start.1
  701.0 12.7 collective-permute-start.1
  714.8 12.7 collective-permute-start.1
  728.7 12.7 collective-permute-start.1
  742.6 12.7 collective-permute-start.1
  756.5 12.7 collective-permute-start.1
  770.3 12.7 collective-permute-start.1
  784.2 12.7 collective-permute-start.1
  798.1 12.7 collective-permute-start.1
  825.8 12.7 collective-permute-start.1
  839.7 12.7 collective-permute-start.1
  853.6 12.7 collective-permute-start.1
  867.5 12.7 collective-permute-start.1
  881.4 12.7 collective-permute-start.1
  895.2 12.7 collective-permute-start.1
  909.1 12.7 collective-permute-start.1
  950.7 12.7 collective-permute-start.1
  964.6 12.7 collective-permute-start.1
  978.5 12.7 collective-permute-start.1
  992.4 12.7 collective-permute-start.1
  1170.0 186.6 %reduce-scatter.8.cloned.1.call-start = ((), (), s32[]{:S(2)}) async-start(), calls=%async_computation.7 | async-start | bytes 4325376 | tf_op jit(solution)/shard_map/reduce_scatter | solution.py:173
  1175.8 276.0 %reduce-scatter.6.cloned.1.call-start = ((), (), s32[]{:S(2)}) async-start(), calls=%async_computation.6 | async-start | bytes 4866048 | tf_op jit(solution)/shard_map/reduce_scatter | solution.py:176
  1216.3 236.2 %all-to-all-start.2 = ((bf16[32,16,1024]{2,1,0:T(8,128)(2,1)}), bf16[32,16,1024]{2,1,0:T(8,128)(2,1)}, u32[]{:S(2)}, u32[]{:S(2)}) async-start(bf16[32,16,1024]{2,1,0:T(8,128)(2,1)} %broadcast_select_fusion.1), calls=%async_computation.2 | async-start | bytes 2097152 | tf_op jit(solution)/shard_map/all_to_all | solution.py:162
  1224.6 302.2 %all-reduce.6.cloned.1.call-start = ((), (), s32[]{:S(2)}) async-start(), calls=%async_computation.9 | async-start | bytes 557056 | tf_op jit(solution)/shard_map/psum | solution.py:179
  (75 other events, 550.0 us)
Sparse Core Ops, SparseCore 0:
  1170.1 93.5 reduce-scatter.9
  1267.7 88.9 reduce-scatter.7
  1361.2 90.5 reduce-scatter.5
  1454.1 72.6 all-reduce.5
where the time goes:
time: 1550 us; the launch traced here: 1540 us
  waiting for transfers between devices  834 us (54%)
  starting transfers between devices  257 us (17%)
  local copies, waits for them, and re-layouts  143 us (9%)
  other arithmetic  141 us (9%)
  matrix products  105 us (7%)
  blocking collectives  40.2 us (3%)
    ppermute x62, waiting for transfers between devices, passed_along(): return lax.ppermute(value, axis, pairs)  544 us
    ppermute x62, starting transfers between devices, passed_along(): return lax.ppermute(value, axis, pairs)  242 us
    reduce_scatter x1, waiting for transfers between devices, local(): lax.psum_scatter(column_term(scan_tokens, grad_proj), 'seq', scatter_dime...  95.2 us
    reduce_scatter x1, waiting for transfers between devices, local(): lax.psum_scatter(out_term, 'seq', scatter_dimension=1, tiled=True)  74.4 us
    psum x1, waiting for transfers between devices, local(): lax.psum((proj_part, out_part, delta_part), 'dp')  71.3 us
    dot_general x6, matrix products, span_step(): inside = jnp.einsum('hts,shp->thp', mixing, values, precision=HIGHEST)  38.3 us
    unnamed x5, waiting for transfers between devices  37.5 us
    add x31, other arithmetic, relay_grad(): return passed_along(outgoing + keep[:, None, None] * passing, 'seq', -1)  35.7 us
  transfers between devices with their start and end apart: 68, of which 67 were waited for; matrix products, arithmetic and copies ran while one was open for 4% of the time, Pallas kernels for 0%

commit v1 on v0

v1 whole, which is shorter than its diff:
```python
import functools

import jax
import jax.numpy as jnp
from jax import lax
from jax.experimental import pallas as pl
from jax.experimental.pallas import tpu as pltpu
from jax.sharding import PartitionSpec as P

H = 16
P_SIZE = 64
N = 64
D = 1024
PROJ = 1152
BLK = 16
NSEQ = 32
NDP = 8
T = 512
L = 128
NC = T // L
EPSILON = 1e-05
F32 = jnp.float32
BF16 = jnp.bfloat16
MESH = pl.DeviceIdType.MESH
VMEM_LIMIT = 48 * 1024 * 1024

VM = pl.BlockSpec(memory_space=pltpu.VMEM)
SM = pl.BlockSpec(memory_space=pltpu.SMEM)

NN = (((1,), (0,)), ((), ()))
NT = (((1,), (1,)), ((), ()))
TN = (((0,), (0,)), ((), ()))


def dot(a, b, dims=NN):
    return lax.dot_general(a, b, dims, preferred_element_type=F32)


def split2(a):
    hi = a.astype(BF16)
    return hi, (a - hi.astype(F32)).astype(BF16)


def split3(a):
    hi, mid = split2(a)
    low = a - hi.astype(F32) - mid.astype(F32)
    return hi, mid, low.astype(BF16)


def dot_exact_right(a, b, dims=NN):
    hi, lo = split2(a)
    return dot(hi, b, dims) + dot(lo, b, dims)


def dot_exact_left3(a, b):
    hi, mid, low = split3(b)
    return (dot(a, low) + dot(a, mid)) + dot(a, hi)


def wide_dot(a, b, dims=NN):
    ka, kb = dims[0][0][0], dims[0][1][0]
    ah, al = split2(a)
    bh, bl = split2(b)
    return dot(
        jnp.concatenate([ah, al, ah], axis=ka), jnp.concatenate([bh, bh, bl], axis=kb), dims
    )


def three_dots(a, b, dims=NN):
    ah, al = split2(a)
    bh, bl = split2(b)
    return (dot(al, bh, dims) + dot(ah, bl, dims)) + dot(ah, bh, dims)


def iota(shape, dim):
    return lax.broadcasted_iota(jnp.int32, shape, dim)


def head_rows():
    return ((iota((H, D), 1) >> 6) == iota((H, D), 0)).astype(F32).astype(BF16)


def head_columns():
    return ((iota((D, H), 0) >> 6) == iota((D, H), 1)).astype(F32).astype(BF16)


def lower_ones():
    return (iota((L, L), 0) >= iota((L, L), 1)).astype(F32).astype(BF16)


def upper_ones():
    return (iota((L, L), 0) <= iota((L, L), 1)).astype(F32).astype(BF16)


def softplus(v):
    return jnp.maximum(v, 0.0) + jnp.log1p(jnp.exp(-jnp.abs(v)))


def sigmoid(v):
    e = jnp.exp(-jnp.abs(v))
    return jnp.where(v >= 0, 1.0, e) / (1.0 + e)


def ids(k):
    z = lax.axis_index("dp")
    me = lax.axis_index("seq")
    return z, me, lax.rem(me + k, NSEQ), lax.rem(me - k + NSEQ, NSEQ)


def greet_all():
    z = lax.axis_index("dp")
    me = lax.axis_index("seq")
    barrier = pltpu.get_barrier_semaphore()

    def hello(k, _):
        pl.semaphore_signal(
            barrier, inc=1, device_id=(z, lax.rem(me + k, NSEQ)), device_id_type=MESH
        )
        return 0

    lax.fori_loop(1, NSEQ, hello, 0)
    pl.semaphore_wait(barrier, NSEQ - 1)


def to_peer(src, dst, send_sem, recv_sem, peer):
    return pltpu.make_async_remote_copy(
        src_ref=src, dst_ref=dst, send_sem=send_sem, recv_sem=recv_sem,
        device_id=peer, device_id_type=MESH,
    )


def scatter_blocks(send, recv, send_sem, recv_sem):
    me = lax.axis_index("seq")

    def go(k, _):
        z, _, to, _ = ids(k)
        to_peer(send.at[to], recv.at[me], send_sem.at[to], recv_sem.at[me], (z, to)).start()
        return 0

    lax.fori_loop(1, NSEQ, go, 0)


def await_blocks(send, recv, send_sem, recv_sem):
    def done(k, _):
        z, _, to, frm = ids(k)
        copy = to_peer(send.at[to], recv.at[frm], send_sem.at[to], recv_sem.at[frm], (z, to))
        copy.wait_send()
        copy.wait_recv()
        return 0

    lax.fori_loop(1, NSEQ, done, 0)


def enter_kernel(src_ref, dst_ref, tok_ref, grad_ref, x_ref, g_ref,
                 send_t, send_g, recv_t, recv_g, st, rt, sg, rg):
    me = lax.axis_index("seq")

    def load_t(d, _):
        send_t[d] = tok_ref[src_ref[0, d]]
        return 0

    def load_g(d, _):
        send_g[d] = grad_ref[src_ref[0, d]]
        return 0

    lax.fori_loop(0, NSEQ, load_t, 0)
    greet_all()
    scatter_blocks(send_t, recv_t, st, rt)
    lax.fori_loop(0, NSEQ, load_g, 0)
    scatter_blocks(send_g, recv_g, sg, rg)
    recv_t[me] = send_t[me]
    recv_g[me] = send_g[me]
    await_blocks(send_t, recv_t, st, rt)

    def settle_t(j, _):
        x_ref[j] = recv_t[dst_ref[0, j]]
        return 0

    lax.fori_loop(0, NSEQ, settle_t, 0)
    await_blocks(send_g, recv_g, sg, rg)

    def settle_g(j, _):
        g_ref[j] = recv_g[dst_ref[0, j]]
        return 0

    lax.fori_loop(0, NSEQ, settle_g, 0)


def enter(tokens, grads, src, dst):
    shape = (NSEQ, BLK, D)
    block = pltpu.VMEM(shape, BF16)
    sems = pltpu.SemaphoreType.DMA((NSEQ,))
    return pl.pallas_call(
        enter_kernel,
        out_shape=[jax.ShapeDtypeStruct(shape, BF16)] * 2,
        in_specs=[SM, SM, VM, VM],
        out_specs=[VM, VM],
        scratch_shapes=[block] * 4 + [sems] * 4,
        compiler_params=pltpu.CompilerParams(
            collective_id=0, has_side_effects=True, vmem_limit_bytes=VMEM_LIMIT
        ),
        name="enter",
    )(src, dst, tokens, grads)


def leave_kernel(inv_ref, ret_ref, out_ref, recv, ss, rs):
    me = lax.axis_index("seq")
    greet_all()
    scatter_blocks(ret_ref, recv, ss, rs)
    recv[me] = ret_ref[me]
    await_blocks(ret_ref, recv, ss, rs)

    def settle(j, _):
        out_ref[j] = recv[inv_ref[0, j]]
        return 0

    lax.fori_loop(0, NSEQ, settle, 0)


def leave(inverse, returning):
    shape = (NSEQ, BLK, D)
    sems = pltpu.SemaphoreType.DMA((NSEQ,))
    return pl.pallas_call(
        leave_kernel,
        out_shape=jax.ShapeDtypeStruct(shape, BF16),
        in_specs=[SM, VM],
        out_specs=VM,
        scratch_shapes=[pltpu.VMEM(shape, BF16), sems, sems],
        compiler_params=pltpu.CompilerParams(
            collective_id=1, has_side_effects=True, vmem_limit_bytes=VMEM_LIMIT
        ),
        name="leave",
    )(inverse, returning)


def relay_kernel(reverse, pay_ref, out_ref, recv, mid, s1, r1, s2, r2):
    me = lax.axis_index("seq")
    greet_all()
    scatter_blocks(pay_ref, recv, s1, r1)
    recv[me] = pay_ref[me]
    await_blocks(pay_ref, recv, s1, r1)

    def step(i, state):
        j = NSEQ - 1 - i if reverse else i
        mid[j] = state
        return recv[j, 8:16] * state + recv[j, 0:8]

    lax.fori_loop(0, NSEQ, step, jnp.zeros((8, 256), F32))
    scatter_blocks(mid, out_ref, s2, r2)
    out_ref[me] = mid[me]
    await_blocks(mid, out_ref, s2, r2)


def relay(payload, reverse):
    sems = pltpu.SemaphoreType.DMA((NSEQ,))
    shape = (NSEQ, 8, 256)
    return pl.pallas_call(
        functools.partial(relay_kernel, reverse),
        out_shape=jax.ShapeDtypeStruct(shape, F32),
        in_specs=[VM],
        out_specs=VM,
        scratch_shapes=[
            pltpu.VMEM((NSEQ, 16, 256), F32), pltpu.VMEM(shape, F32), sems, sems, sems, sems
        ],
        compiler_params=pltpu.CompilerParams(
            collective_id=3 if reverse else 2, has_side_effects=True,
            vmem_limit_bytes=VMEM_LIMIT,
        ),
        name="relay_back" if reverse else "relay",
    )(payload)


def pack_payload(pay_ref, state, keep):
    for rg in range(8):
        for lg in range(4):
            lanes = slice(256 * lg, 256 * lg + 256)
            pay_ref[rg * 4 + lg, 0:8, :] = state[8 * rg:8 * rg + 8, lanes]
            pay_ref[rg * 4 + lg, 8:16, :] = jnp.broadcast_to(keep[:, lanes], (8, 256))


def unpack_state(ref, state_ref):
    for rg in range(8):
        for lg in range(4):
            state_ref[8 * rg:8 * rg + 8, 256 * lg:256 * lg + 256] = ref[rg * 4 + lg]


def project_kernel(x_ref, wp_ref, wd_ref, bias_ref, rate_ref,
                   v_ref, bc_ref, raw_ref, run_ref, runt_ref, u_ref, pay_ref):
    heads = head_rows()
    lower = lower_ones()
    bias = bias_ref[...]
    rate = rate_ref[...]

    def chunk(c, carry):
        state, total = carry
        rows = pl.ds(pl.multiple_of(c * L, L), L)
        x = x_ref[rows, :]
        v = dot(x, wp_ref[:, 0:D])
        v_ref[rows, :] = v
        bc = dot(x, wp_ref[:, D:PROJ])
        bc_ref[rows, :] = bc
        raw = dot(x, wd_ref[...]) + bias
        raw_ref[rows, :] = raw
        delta = softplus(raw)
        running = dot_exact_left3(lower, -rate * delta)
        run_ref[rows, :] = running
        runt_ref[c] = running.T
        last = running[L - 1:L, :]
        weight = jnp.exp(last - running) * delta
        weighted = v * dot_exact_right(weight, heads)
        added = wide_dot(bc[:, 0:N], weighted, TN)
        u_ref[c] = added
        keep = dot_exact_right(jnp.broadcast_to(jnp.exp(last), (8, H)), heads)[0:1]
        return keep * state + added, total + last

    state, total = lax.fori_loop(
        0, NC, chunk, (jnp.zeros((N, D), F32), jnp.zeros((1, H), F32))
    )
    hi, mid, low = split3(jnp.broadcast_to(jnp.exp(total), (8, H)))
    keep = (dot(low, heads) + dot(mid, heads)) + dot(hi, heads)
    pack_payload(pay_ref, state, keep[0:1])


def project(x, w_proj, w_dt, bias, rate):
    return pl.pallas_call(
        project_kernel,
        out_shape=[
            jax.ShapeDtypeStruct((T, D), F32),
            jax.ShapeDtypeStruct((T, 2 * N), F32),
            jax.ShapeDtypeStruct((T, H), F32),
            jax.ShapeDtypeStruct((T, H), F32),
            jax.ShapeDtypeStruct((NC, H, L), F32),
            jax.ShapeDtypeStruct((NC, N, D), F32),
            jax.ShapeDtypeStruct((NSEQ, 16, 256), F32),
        ],
        in_specs=[VM] * 5,
        out_specs=[VM] * 7,
        compiler_params=pltpu.CompilerParams(vmem_limit_bytes=VMEM_LIMIT),
        name="project",
    )(x, w_proj, w_dt, bias, rate)


def forward_kernel(ent_ref, v_ref, bc_ref, raw_ref, run_ref, runt_ref, u_ref, g_ref, wo_ref,
                   skip_ref, gain_ref,
                   dy_ref, low_ref, q_ref, dc_ref, s_ref, r_ref, pay_ref, state_ref):
    heads = head_rows()
    cols = head_columns()
    lanes = iota((1, 128), 1)
    even = lanes < 64
    skip = dot_exact_right(jnp.broadcast_to(skip_ref[...], (8, H)), heads)[0:1]
    gain = gain_ref[...]
    unpack_state(ent_ref, state_ref)
    below = iota((L, L), 0) >= iota((L, L), 1)

    def chunk(c, carry):
        out_grad, before, total = carry
        rows = pl.ds(pl.multiple_of(c * L, L), L)
        v = v_ref[rows, :]
        bc = bc_ref[rows, :]
        b, r = bc[:, 0:N], bc[:, N:2 * N]
        delta = softplus(raw_ref[rows, :])
        running = run_ref[rows, :]
        runt = runt_ref[c]
        last = running[L - 1:L, :]
        state = state_ref[...]
        s_ref[c] = state
        grown = dot_exact_right(jnp.exp(running), heads)
        carried = wide_dot(r, state) * grown
        scaled = (v * dot_exact_right(delta, heads)).astype(BF16)
        scores = wide_dot(r, b, NT)
        inside = []
        for j in range(H // 2):
            mixes = []
            for h in (2 * j, 2 * j + 1):
                spread = running[:, h:h + 1] - runt[h:h + 1, :]
                decay = jnp.exp(jnp.where(below, spread, -jnp.inf))
                mixes.append((decay * scores).astype(BF16))
            pair = scaled[:, 128 * j:128 * j + 128]
            zero = jnp.zeros_like(pair)
            stacked = jnp.concatenate(
                [jnp.where(even, pair, zero), jnp.where(even, zero, pair)], axis=0
            )
            inside.append(dot(jnp.concatenate(mixes, axis=1), stacked))
        summed = jnp.concatenate(inside, axis=1) + carried + skip * v
        square = dot_exact_right(summed * summed, cols) * (1.0 / P_SIZE)
        scale = dot_exact_right(lax.rsqrt(square + EPSILON), heads)
        unit = summed * scale
        low_ref[rows, :] = (unit * gain).astype(BF16)
        grad_unit = dot(g_ref[rows, :], wo_ref[...], NT) * gain
        along = dot_exact_right(grad_unit * unit, cols) * (1.0 / P_SIZE)
        dy = scale * (grad_unit - unit * dot_exact_right(along, heads))
        dy_ref[rows, :] = dy
        q_ref[rows, :] = dot_exact_right(dy * carried, cols)
        back = dy * grown
        dc_ref[rows, :] = three_dots(back, state, NT)
        reach = wide_dot(r, back, TN)
        r_ref[c] = reach
        keep = dot_exact_right(jnp.broadcast_to(jnp.exp(last), (8, H)), heads)[0:1]
        state_ref[...] = keep * state + u_ref[c]
        return out_grad + before * reach, before * keep, total + last

    out_grad, _, total = lax.fori_loop(
        0, NC, chunk,
        (jnp.zeros((N, D), F32), jnp.ones((1, D), F32), jnp.zeros((1, H), F32)),
    )
    hi, mid, low = split3(jnp.broadcast_to(jnp.exp(total), (8, H)))
    keep = (dot(low, heads) + dot(mid, heads)) + dot(hi, heads)
    pack_payload(pay_ref, out_grad, keep[0:1])


def forward(entering, v, bc, raw, run, runt, u, g, w_out, skip, gain):
    return pl.pallas_call(
        forward_kernel,
        out_shape=[
            jax.ShapeDtypeStruct((T, D), F32),
            jax.ShapeDtypeStruct((T, D), BF16),
            jax.ShapeDtypeStruct((T, H), F32),
            jax.ShapeDtypeStruct((T, N), F32),
            jax.ShapeDtypeStruct((NC, N, D), F32),
            jax.ShapeDtypeStruct((NC, N, D), F32),
            jax.ShapeDtypeStruct((NSEQ, 16, 256), F32),
        ],
        in_specs=[VM] * 11,
        out_specs=[VM] * 7,
        scratch_shapes=[pltpu.VMEM((N, D), F32)],
        compiler_params=pltpu.CompilerParams(vmem_limit_bytes=VMEM_LIMIT),
        name="forward",
    )(entering, v, bc, raw, run, runt, u, g, w_out, skip, gain)


def backward_kernel(src_ref, dst_ref, lv_ref, x_ref, g_ref, v_ref, bc_ref, raw_ref, run_ref,
                    runt_ref, dy_ref, low_ref, q_ref, dc_ref, s_ref, r_ref,
                    wp_ref, wd_ref, rate_ref, skip_ref,
                    ret_ref, inv_ref, p1_ref, p2_ref,
                    grad_ref, gp_ref, gd_ref):
    heads = head_rows()
    cols = head_columns()
    upper = upper_ones()
    even = iota((1, 128), 1) < 64
    skip = dot_exact_right(jnp.broadcast_to(skip_ref[...], (8, H)), heads)[0:1]
    rate = rate_ref[...]
    unpack_state(lv_ref, grad_ref)
    after = iota((L, L), 1) >= iota((L, L), 0)
    half = iota((2 * L, H), 0) >> 7
    pick = iota((2 * L, H), 1)
    halft = iota((H, 2 * L), 1) >> 7
    pickt = iota((H, 2 * L), 0)

    def invert(d, _):
        inv_ref[0, src_ref[0, d]] = d
        return 0

    lax.fori_loop(0, NSEQ, invert, 0)

    def chunk(i, _):
        c = NC - 1 - i
        rows = pl.ds(pl.multiple_of(c * L, L), L)
        v = v_ref[rows, :]
        bc = bc_ref[rows, :]
        b, r = bc[:, 0:N], bc[:, N:2 * N]
        raw = raw_ref[rows, :]
        delta = softplus(raw)
        running = run_ref[rows, :]
        runt = runt_ref[c]
        last = running[L - 1:L, :]
        dy = dy_ref[rows, :]
        dy_low = dy.astype(BF16)
        grad = grad_ref[...]
        widened = dot_exact_right(delta, heads)
        scaled = v * widened
        scaled_low = scaled.astype(BF16)
        fade = dot_exact_right(jnp.exp(last - running), heads)
        weighted = scaled * fade
        d_weighted = wide_dot(b, grad)
        used = dot_exact_right(d_weighted * weighted, cols)
        db = three_dots(weighted, grad, NT)
        keep = dot_exact_right(jnp.broadcast_to(jnp.exp(last), (8, H)), heads)[0:1]
        held = jnp.sum(keep * grad * s_ref[c], axis=0, keepdims=True)
        held = dot_exact_right(jnp.broadcast_to(held, (8, D)), cols)[0:1]
        scores_t = wide_dot(b, r, NT)
        dscores_t = jnp.zeros((L, L), F32)
        by_source = jnp.zeros((L, H), F32)
        by_target = jnp.zeros((H, L), F32)
        inside = []
        for j in range(H // 2):
            pair = slice(128 * j, 128 * j + 128)
            sp = scaled_low[:, pair]
            dp = dy_low[:, pair]
            zero = jnp.zeros_like(sp)
            mixes, flows = [], []
            for e in (0, 1):
                h = 2 * j + e
                spread = runt[h:h + 1, :] - running[:, h:h + 1]
                decay = jnp.exp(jnp.where(after, spread, -jnp.inf))
                mixes.append((decay * scores_t).astype(BF16))
                mine = jnp.where(even, sp, zero) if e == 0 else jnp.where(even, zero, sp)
                moved = dot(mine, dp, NT) * decay
                dscores_t = dscores_t + moved
                flows.append((moved * scores_t).astype(BF16))
            stacked = jnp.concatenate(
                [jnp.where(even, dp, zero), jnp.where(even, zero, dp)], axis=0
            )
            inside.append(dot(jnp.concatenate(mixes, axis=1), stacked))
            which = (pick == 2 * j + half).astype(F32).astype(BF16)
            which_t = (pickt == 2 * j + halft).astype(F32).astype(BF16)
            by_source = by_source + dot(jnp.concatenate(flows, axis=1), which)
            by_target = by_target + dot(which_t, jnp.concatenate(flows, axis=0))
        d_scaled = d_weighted * fade + jnp.concatenate(inside, axis=1)
        db = db + three_dots(dscores_t, r)
        dc = dc_ref[rows, :] + three_dots(dscores_t, b, TN)
        d_running = by_target.T - by_source + q_ref[rows, :] - used
        d_last = jnp.sum(used, axis=0, keepdims=True) + held
        d_decay = dot_exact_left3(upper, d_running) + d_last
        d_delta = dot_exact_right(d_scaled * v, cols) - rate * d_decay
        gd_ref[rows, :] = (d_delta * sigmoid(raw)).astype(BF16)
        gp_ref[rows, 0:D] = (d_scaled * widened + skip * dy).astype(BF16)
        gp_ref[rows, D:PROJ] = jnp.concatenate([db, dc], axis=1).astype(BF16)
        grad_ref[...] = r_ref[c] + keep * grad
        return 0

    lax.fori_loop(0, NC, chunk, 0)

    def send_back(c, _):
        rows = pl.ds(pl.multiple_of(c * L, L), L)
        gs = dot(gp_ref[rows, :], wp_ref[...], NT) + dot(gd_ref[rows, :], wd_ref[...], NT)
        gs = gs.astype(BF16)
        for k in range(L // BLK):
            ret_ref[dst_ref[0, c * (L // BLK) + k]] = gs[BLK * k:BLK * k + BLK]
        return 0

    lax.fori_loop(0, NC, send_back, 0)

    gp = gp_ref[...]
    gd = gd_ref[...]
    low = low_ref[...]
    for m in range(8):
        lanes = slice(128 * m, 128 * m + 128)
        xt = x_ref[:, lanes].T
        gt = g_ref[:, lanes].T
        proj_rows = dot(xt, gp).astype(BF16)
        out_rows = dot(gt, low).astype(BF16)
        dt_rows = dot(xt, gd)
        dt_hi, dt_lo = split2(dt_rows)
        dt_rows = jnp.concatenate([dt_hi, dt_lo, jnp.zeros((128, 128 - 2 * H), BF16)], axis=1)
        for k in range(4):
            d = 4 * m + k
            y, xx, core = d >> 3, (d >> 1) & 3, d & 1
            sub = slice(32 * k, 32 * k + 32)
            p1_ref[core, xx, y] = proj_rows[sub]
            p2_ref[core, y, xx, :, 0:D] = out_rows[sub]
            p2_ref[core, y, xx, :, D:PROJ] = dt_rows[sub]


def backward(src, dst, leaving, x, g, v, bc, raw, run, runt, dy, low, q, dc, s, r,
             w_proj, w_dt, rate, skip):
    part = jax.ShapeDtypeStruct((2, 4, 4, 32, PROJ), BF16)
    return pl.pallas_call(
        backward_kernel,
        out_shape=[
            jax.ShapeDtypeStruct((NSEQ, BLK, D), BF16),
            jax.ShapeDtypeStruct((1, NSEQ), jnp.int32),
            part,
            part,
        ],
        in_specs=[SM, SM] + [VM] * 18,
        out_specs=[VM, SM, VM, VM],
        scratch_shapes=[
            pltpu.VMEM((N, D), F32), pltpu.VMEM((T, PROJ), BF16), pltpu.VMEM((T, H), BF16)
        ],
        compiler_params=pltpu.CompilerParams(vmem_limit_bytes=VMEM_LIMIT),
        name="backward",
    )(src, dst, leaving, x, g, v, bc, raw, run, runt, dy, low, q, dc, s, r,
      w_proj, w_dt, rate, skip)


def places():
    z = lax.axis_index("dp")
    me = lax.axis_index("seq")
    y = me // 8
    x = lax.rem(me // 2, 4)
    core = lax.rem(me, 2)
    return z, y, x, core


def narrow(total):
    return total.astype(BF16)


def narrow_pairs(total):
    tail = total[:, D:PROJ]
    high = tail.astype(BF16).astype(F32)
    rest = (tail - high)[:, 0:H]
    width = tail.shape[1]
    moved = jnp.concatenate(
        [jnp.zeros_like(rest), rest, jnp.zeros((rest.shape[0], width - 2 * H), F32)], axis=1
    )
    lane = iota(tail.shape, 1)
    tail = jnp.where(lane < H, high, tail + moved)
    return jnp.concatenate([total[:, 0:D], tail], axis=1).astype(BF16)


def reduce_kernel(p1_ref, p2_ref, gp_ref, gd_ref, go_ref,
                  ra1, ra2, t1, t2, rb1, rb2, h1, h2, rc1, rc2, zs, zr, zo,
                  sa, qa, sb, qb, sc, qc, sz, qz, so, qo):
    z, y, x, core = places()
    seq = 8 * y + 2 * x + core
    partner = (z, seq + 1 - 2 * core)

    def at_x(k):
        return (z, 8 * y + 2 * lax.rem(x + k, 4) + core)

    def at_y(k):
        return (z, 8 * lax.rem(y + k, 4) + 2 * x + core)

    def at_z(k):
        return (lax.rem(z + k, NDP), seq)

    barrier = pltpu.get_barrier_semaphore()
    pl.semaphore_signal(barrier, inc=1, device_id=partner, device_id_type=MESH)
    for k in (1, 2, 3):
        pl.semaphore_signal(barrier, inc=1, device_id=at_x(k), device_id_type=MESH)
        pl.semaphore_signal(barrier, inc=1, device_id=at_y(k), device_id_type=MESH)
    for k in range(1, NDP):
        pl.semaphore_signal(barrier, inc=1, device_id=at_z(k), device_id_type=MESH)
    pl.semaphore_wait(barrier, 14)

    a1 = to_peer(p1_ref.at[1 - core], ra1, sa.at[0], qa.at[0], partner)
    a2 = to_peer(p2_ref.at[1 - core], ra2, sa.at[1], qa.at[1], partner)
    a1.start()
    a2.start()

    def hop(src, dst, send, recv, first, here, place):
        copies = []
        for k in (1, 2, 3):
            to = lax.rem(here + k, 4)
            frm = lax.rem(here - k + 4, 4)
            copies.append((
                to_peer(src.at[to], dst.at[here], send.at[first + to], recv.at[first + here],
                        place(k)),
                to_peer(src.at[to], dst.at[frm], send.at[first + to], recv.at[first + frm],
                        place(k)),
            ))
        return copies

    b1 = hop(t1, rb1, sb, qb, 0, x, at_x)
    b2 = hop(t2, rb2, sb, qb, 4, y, at_y)
    c1 = hop(h1, rc1, sc, qc, 0, y, at_y)
    c2 = hop(h2, rc2, sc, qc, 4, x, at_x)

    def add_pair(p_ref, ra, t, form):
        def body(i, _):
            a, b = i // 4, lax.rem(i, 4)
            t[a, b] = form(p_ref[core, a, b].astype(F32) + ra[a, b].astype(F32))
            return 0

        lax.fori_loop(0, 16, body, 0)

    a1.wait()
    add_pair(p1_ref, ra1, t1, narrow)
    for go, _ in b1:
        go.start()
    a2.wait()
    add_pair(p2_ref, ra2, t2, narrow_pairs)
    for go, _ in b2:
        go.start()

    def first_sum(t, rb, h, here, copies, form):
        for _, got in copies:
            got.wait_send()
            got.wait_recv()

        def body(b, _):
            total = t[here, b].astype(F32)
            for k in (1, 2, 3):
                total = total + rb[lax.rem(here + k, 4), b].astype(F32)
            h[b] = form(total)
            return 0

        lax.fori_loop(0, 4, body, 0)

    first_sum(t1, rb1, h1, x, b1, narrow)
    for go, _ in c1:
        go.start()
    first_sum(t2, rb2, h2, y, b2, narrow_pairs)
    for go, _ in c2:
        go.start()

    def second_sum(h, rc, here, copies):
        for _, got in copies:
            got.wait_send()
            got.wait_recv()
        total = h[here].astype(F32)
        for k in (1, 2, 3):
            total = total + rc[lax.rem(here + k, 4)].astype(F32)
        return total

    s1 = second_sum(h1, rc1, y, c1)
    for i in range(4):
        zs[i] = s1[8 * i:8 * i + 8]
    s2 = second_sum(h2, rc2, x, c2)
    for i in range(4):
        zs[4 + i] = s2[8 * i:8 * i + 8]

    def z_out(k, _):
        to = lax.rem(z + k, NDP)
        to_peer(zs.at[to], zr.at[z], sz.at[to], qz.at[z], at_z(k)).start()
        return 0

    lax.fori_loop(1, NDP, z_out, 0)

    def z_done(k, total):
        to = lax.rem(z + k, NDP)
        frm = lax.rem(z - k + NDP, NDP)
        copy = to_peer(zs.at[to], zr.at[frm], sz.at[to], qz.at[frm], at_z(k))
        copy.wait_send()
        copy.wait_recv()
        return total + zr[frm]

    total = lax.fori_loop(1, NDP, z_done, zs[z])
    zo[z] = total * ((NDP * NSEQ * T) ** (-0.5))

    def o_out(k, _):
        to_peer(zo.at[z], zo.at[z], so.at[k], qo.at[z], at_z(k)).start()
        return 0

    lax.fori_loop(1, NDP, o_out, 0)

    def o_done(k, _):
        frm = lax.rem(z - k + NDP, NDP)
        copy = to_peer(zo.at[z], zo.at[frm], so.at[k], qo.at[frm], at_z(k))
        copy.wait_send()
        copy.wait_recv()
        return 0

    lax.fori_loop(1, NDP, o_done, 0)
    for i in range(4):
        gp_ref[8 * i:8 * i + 8, :] = zo[i]
        gd_ref[8 * i:8 * i + 8, :] = zo[4 + i, :, D:PROJ]
        go_ref[8 * i:8 * i + 8, :] = zo[4 + i, :, 0:D]


def reduce_all(p1, p2):
    part = pltpu.VMEM((4, 4, 32, PROJ), BF16)
    line = pltpu.VMEM((4, 32, PROJ), BF16)
    zed = pltpu.VMEM((NDP, 8, PROJ), F32)
    dma = pltpu.SemaphoreType.DMA
    return pl.pallas_call(
        reduce_kernel,
        out_shape=[
            jax.ShapeDtypeStruct((32, PROJ), F32),
            jax.ShapeDtypeStruct((32, 128), F32),
            jax.ShapeDtypeStruct((32, D), F32),
        ],
        in_specs=[VM] * 2,
        out_specs=[VM] * 3,
        scratch_shapes=[part] * 6 + [line] * 4 + [zed] * 3
        + [dma((2,)), dma((2,)), dma((8,)), dma((8,)), dma((8,)), dma((8,)),
           dma((8,)), dma((8,)), dma((8,)), dma((8,))],
        compiler_params=pltpu.CompilerParams(
            collective_id=4, has_side_effects=True, vmem_limit_bytes=VMEM_LIMIT
        ),
        name="reduce_all",
    )(p1, p2)


def local(tokens, grad_out, src_order, dst_order, w_proj, w_dt, w_out,
          dt_bias, decay_rate, d_skip, norm_gain):
    blocks = (NSEQ, BLK, D)
    bias = dt_bias.reshape(1, H)
    rate = decay_rate.reshape(1, H)
    skip = d_skip.reshape(1, H)
    gain = norm_gain.reshape(1, D)
    x, g = enter(tokens.reshape(blocks), grad_out.reshape(blocks), src_order, dst_order)
    x = x.reshape(T, D)
    g = g.reshape(T, D)
    v, bc, raw, run, runt, u, pay = project(x, w_proj, w_dt, bias, rate)
    entering = relay(pay, False)
    dy, low, q, dc, s, r, pay_back = forward(
        entering, v, bc, raw, run, runt, u, g, w_out, skip, gain
    )
    leaving = relay(pay_back, True)
    returning, inverse, p1, p2 = backward(
        src_order, dst_order, leaving, x, g, v, bc, raw, run, runt, dy, low, q, dc, s, r,
        w_proj, w_dt, rate, skip
    )
    grad_tokens = leave(inverse, returning)
    gp, gd, go = reduce_all(p1, p2)
    return grad_tokens.reshape(1, T, D), gp, gd[:, 0:H] + gd[:, H:2 * H], go.T


def solution(mesh):
    in_specs = (
        P("dp", "seq", None), P("dp", "seq", None), P("seq", None), P("seq", None),
        P(), P(), P(), P(), P(), P(), P(),
    )
    out_specs = (P("dp", "seq", None), P("seq", None), P("seq", None), P(None, "seq"))
    return jax.shard_map(local, mesh=mesh, in_specs=in_specs, out_specs=out_specs, check_vma=False)
```

time: 1550 us -> 213 us (0.14)
  waiting for transfers between devices: 834 us -> 0 us
  starting transfers between devices: 257 us -> 0 us
  Pallas kernels: 0 us -> 193 us
  other arithmetic: 141 us -> 0.07 us
  local copies, waits for them, and re-layouts: 143 us -> 16.2 us
  matrix products: 105 us -> 0 us
  blocking collectives: 40.2 us -> 0 us
    ppermute x62 -> x0, waiting for transfers between devices: 544 us -> none  [passed_along(): return lax.ppermute(value, axis, pairs)]
    ppermute x62 -> x0, starting transfers between devices: 242 us -> none  [passed_along(): return lax.ppermute(value, axis, pairs)]
    pallas_call x0 -> x8, Pallas kernels: none -> 193 us  [the longest x1 52.1 us: reduce_all(): pl.pallas_call(reduce_kernel, out_shape=[jax.ShapeDtypeStruct((32, PROJ),...]
    reduce_scatter x2 -> x0, waiting for transfers between devices: 170 us -> none  [the longest x1 95.2 us: local(): lax.psum_scatter(column_term(scan_tokens, grad_proj), 'seq', scatter_dime...]
    dot_general x37 -> x0, matrix products: 104 us -> none  [the longest x6 38.3 us: span_step(): inside = jnp.einsum('hts,shp->thp', mixing, values, precision=HIGHEST)]
    psum x1 -> x0, waiting for transfers between devices: 71.3 us -> none  [local(): lax.psum((proj_part, out_part, delta_part), 'dp')]
    add x64 -> x1, other arithmetic: 68.3 us -> 0.07 us  [local(): return (grad_tokens.reshape(1, T, D), gp, gd[:, 0:H] + gd[:, H:2 * H], go.T)]
    unnamed x5 -> x0, waiting for transfers between devices: 37.5 us -> none
  transfers between devices with their start and end apart: 68 -> 0, of which waited for: 67 -> 0; matrix products, arithmetic and copies ran while one was open for 4% -> 0% of each run, Pallas kernels for 0% -> 0%
where the time goes in v1:
time: 213 us; the launch traced here: 211 us
  Pallas kernels  193 us (91%)
  local copies, waits for them, and re-layouts  16.2 us (8%)
    pallas_call x1, Pallas kernels, reduce_all(): pl.pallas_call(reduce_kernel, out_shape=[jax.ShapeDtypeStruct((32, PROJ),...  52.1 us
    pallas_call x2, Pallas kernels, relay(): pl.pallas_call(functools.partial(relay_kernel, reverse), out_shape=jax.Sh...  39.8 us
    pallas_call x1, Pallas kernels, enter(): pl.pallas_call(enter_kernel, out_shape=[jax.ShapeDtypeStruct(shape, BF16)...  33.1 us
    pallas_call x1, Pallas kernels, backward(): pl.pallas_call(backward_kernel, out_shape=[jax.ShapeDtypeStruct((NSEQ, BL...  25 us
    pallas_call x1, Pallas kernels, leave(): pl.pallas_call(leave_kernel, out_shape=jax.ShapeDtypeStruct(shape, BF16),...  19.4 us
    pallas_call x1, Pallas kernels, forward(): pl.pallas_call(forward_kernel, out_shape=[jax.ShapeDtypeStruct((T, D), F3...  16.7 us
    unnamed x41, local copies, waits for them, and re-layouts  16.2 us
    pallas_call x1, Pallas kernels, project(): pl.pallas_call(project_kernel, out_shape=[jax.ShapeDtypeStruct((T, D), F3...  7.28 us

profile of v1, /device:TPU:24, one launch (start us, length us, event | category | flops | bytes accessed | tf_op | source)
XLA Modules:
  0.0 210.6 jit_solution(3945446212157180912)
XLA Ops:
  0.6 0.0 copy-start.11
  0.6 0.0 copy-start.17
  0.7 0.9 copy.15.wd_ref
  1.6 0.0 copy-start.8
  1.6 1.2 copy-done.8
  2.8 0.0 copy-start.9
  2.8 1.2 copy-done.9
  4.1 0.0 copy-start.13
  4.1 0.7 copy-done.13
  4.7 0.0 copy-start.15
  4.7 0.7 copy-done.15
  5.4 33.1 %enter.1 = (bf16[32,16,1024]{2,1,0:T(8,128)(2,1)S(1)}, bf16[32,16,1024]{2,1,0:T(8,128)(2,1)S(1)}) custom-call(s32[1,32]{1,0:T(1,128)S(1)} %copy-done.13, s32[1,32]{1,0:T(1,128)S(1)} %copy-done.15, bf16[32,16,1024]{2,1,0:T(8,128)(2,1)S(1)} %bitcast.15, bf16[32,16,1024]{2,1,0:T(8,128)(2,1)S(1)} %bitcast.16), custom_call_target="tpu_custom_call" | custom-call | tf_op jit(solution)/shard_map/enter/pallas_call | solution.py:193
  38.5 0.0 copy-start.1
  38.5 1.0 copy-done.1
  39.5 0.0 copy-start.10
  39.5 0.0 copy-start.12
  39.5 0.0 copy-done.11
  39.5 0.0 copy-done.17
  39.5 7.3 %project.1 = (f32[512,1024]{1,0:T(8,128)S(1)}, f32[512,128]{1,0:T(8,128)S(1)}, f32[512,16]{1,0:T(8,128)S(1)}, f32[512,16]{1,0:T(8,128)S(1)}, f32[4,16,128]{2,1,0...) custom-call(bf16[512,1024]{1,0:T(8,128)(2,1)S(1)} %bitcast.13, bf16[1024,1152]{1,0:T(8,128)(2,1)} %wp_ref.3, ...), custom_call_target="tpu_custom_call" | custom-call | tf_op jit(solution)/shard_map/project/pallas_call | solution.py:325
  46.8 0.0 copy-start
  46.8 1.3 copy-done
  48.1 0.0 copy-start.7
  48.1 1.0 copy-done.7
  49.1 20.2 %relay.1.ent_ref = f32[32,8,256]{2,1,0:T(8,128)S(1)} custom-call(f32[32,16,256]{2,1,0:T(8,128)S(1)} %get-tuple-element.28.pay_ref), custom_call_target="tpu_custom_call" | custom-call | tf_op jit(solution)/shard_map/relay/pallas_call | solution.py:257
  69.3 0.0 copy-done.10
  69.3 0.0 copy-done.12
  69.3 0.0 copy-start.2
  69.3 0.0 copy-start.14
  69.3 0.0 copy-start.16
  69.3 16.7 %forward.1 = (f32[512,1024]{1,0:T(8,128)}, bf16[512,1024]{1,0:T(8,128)(2,1)S(1)}, f32[512,16]{1,0:T(8,128)S(1)}, f32[512,64]{1,0:T(8,128)S(1)}, f32[4,64,1024]{2...) custom-call(f32[32,8,256]{2,1,0:T(8,128)S(1)} %relay.1.ent_ref, f32[512,1024]{1,0:T(8,128)} %copy-done, ...), custom_call_target="tpu_custom_call" | custom-call | tf_op jit(solution)/shard_map/forward/pallas_call | solution.py:412
  86.1 0.0 copy-start.5
  86.1 1.0 copy-done.5
  87.0 0.0 copy-start.6
  87.0 1.0 copy-done.6
  88.0 19.6 %relay_back.1.lv_ref = f32[32,8,256]{2,1,0:T(8,128)S(1)} custom-call(f32[32,16,256]{2,1,0:T(8,128)S(1)} %get-tuple-element.36.pay_ref), custom_call_target="tpu_custom_call" | custom-call | tf_op jit(solution)/shard_map/relay_back/pallas_call | solution.py:257
  107.6 0.0 copy-done.2
  107.6 0.0 copy-done.14
  107.6 0.0 copy-done.16
  107.7 25.0 %backward.1 = (bf16[32,16,1024]{2,1,0:T(8,128)(2,1)S(1)}, s32[1,32]{1,0:T(1,128)S(1)}, bf16[2,4,4,32,1152]{4,3,2,1,0:T(8,128)(2,1)}, bf16[2,4,4,32,1152]{4,3,2,1,0:T(8,128)(2,1)}) custom-call(s32[1,32]{1,0:T(1,128)S(1)} %copy-done.14, s32[1,32]{1,0:T(1,128)S(1)} %copy-done.16, f32[32,8,256]{2,1,0:T(8,128)S(1)} %relay_back.1.lv_ref, ...), custom_call_target="tpu_custom_call" | custom-call | tf_op jit(solution)/shard_map/backward/pallas_call | solution.py:557
  132.6 19.4 %leave.1 = bf16[32,16,1024]{2,1,0:T(8,128)(2,1)S(1)} custom-call(s32[1,32]{1,0:T(1,128)S(1)} %get-tuple-element.43.inv_ref, bf16[32,16,1024]{2,1,0:T(8,128)(2,1)S(1)} %get-tuple-element.44.ret_ref), custom_call_target="tpu_custom_call" | custom-call | tf_op jit(solution)/shard_map/leave/pallas_call | solution.py:223
  152.1 0.0 copy-start.3
  152.1 1.7 copy-done.3
  153.7 0.0 copy-start.4
  153.8 1.7 copy-done.4
  155.4 52.1 %reduce_all.1 = (f32[32,1152]{1,0:T(8,128)S(1)}, f32[32,128]{1,0:T(8,128)S(1)}, f32[32,1024]{1,0:T(8,128)S(1)}) custom-call(bf16[2,4,4,32,1152]{4,3,2,1,0:T(8,128)(2,1)S(1)} %copy-done.3, bf16[2,4,4,32,1152]{4,3,2,1,0:T(8,128)(2,1)S(1)} %copy-done.4), custom_call_target="tpu_custom_call" | custom-call | tf_op jit(solution)/shard_map/reduce_all/pallas_call | solution.py:747
  207.5 0.1 slice_add_fusion
  207.6 0.7 copy.17
  208.3 1.0 copy.21
  209.3 0.7 copy.22
  209.9 0.7 copy.23
Async XLA Ops:
  0.6 38.9 %copy-start.11 = (f32[16]{0:T(128)S(1)}, f32[16]{0:T(128)}, u32[]{:S(2)}) copy-start(f32[16]{0:T(128)} %param.19) | copy-start | bytes 196
  0.6 38.8 %copy-start.17 = (f32[16]{0:T(128)S(1)}, f32[16]{0:T(128)}, u32[]{:S(2)}) copy-start(f32[16]{0:T(128)} %param.18) | copy-start | bytes 196
  1.6 1.2 copy-start.8
  2.8 1.2 copy-start.9
  4.1 0.7 copy-start.13
  4.7 0.7 copy-start.15
  38.5 1.0 copy-start.1
  39.5 29.8 %copy-start.10 = (f32[1024]{0:T(1024)S(1)}, f32[1024]{0:T(1024)}, u32[]{:S(2)}) copy-start(f32[1024]{0:T(1024)} %param.21) | copy-start | bytes 12292
  39.5 29.8 %copy-start.12 = (f32[16]{0:T(128)S(1)}, f32[16]{0:T(128)}, u32[]{:S(2)}) copy-start(f32[16]{0:T(128)} %param.20) | copy-start | bytes 196
  46.8 1.4 copy-start
  48.1 1.0 copy-start.7
  69.3 38.3 %copy-start.2 = (bf16[32,16,1024]{2,1,0:T(8,128)(2,1)S(1)}, bf16[32,16,1024]{2,1,0:T(8,128)(2,1)}, u32[]{:S(2)}) copy-start(bf16[32,16,1024]{2,1,0:T(8,128)(2,1)} %copy-done.1) | copy-start | bytes 3145732
  69.3 38.3 %copy-start.14 = (s32[1,32]{1,0:T(1,128)S(1)}, s32[1,32]{1,0:T(1,128)}, u32[]{:S(2)}) copy-start(s32[1,32]{1,0:T(1,128)} %src_ref.3) | copy-start | bytes 388
  69.3 38.3 %copy-start.16 = (s32[1,32]{1,0:T(1,128)S(1)}, s32[1,32]{1,0:T(1,128)}, u32[]{:S(2)}) copy-start(s32[1,32]{1,0:T(1,128)} %dst_ref.3) | copy-start | bytes 388
  86.1 1.0 copy-start.5
  87.0 1.0 copy-start.6
  152.1 1.7 copy-start.3
  153.7 1.7 copy-start.4

commit v2 on v0

v2 whole, which is shorter than its diff:
```python
import functools

import jax
import jax.numpy as jnp
from jax import lax
from jax.experimental import pallas as pl
from jax.experimental.pallas import tpu as pltpu
from jax.sharding import PartitionSpec as P

H = 16
P_SIZE = 64
N = 64
D = 1024
PROJ = 1152
BLK = 16
NSEQ = 32
NDP = 8
T = 512
L = 128
NC = T // L
EPSILON = 1e-05
F32 = jnp.float32
BF16 = jnp.bfloat16
MESH = pl.DeviceIdType.MESH
VMEM_LIMIT = 62 * 1024 * 1024
HALF = 640

VM = pl.BlockSpec(memory_space=pltpu.VMEM)
SM = pl.BlockSpec(memory_space=pltpu.SMEM)

NN = (((1,), (0,)), ((), ()))
NT = (((1,), (1,)), ((), ()))
TN = (((0,), (0,)), ((), ()))


def dot(a, b, dims=NN):
    return lax.dot_general(a, b, dims, preferred_element_type=F32)


def split2(a):
    hi = a.astype(BF16)
    return hi, (a - hi.astype(F32)).astype(BF16)


def split3(a):
    hi, mid = split2(a)
    low = a - hi.astype(F32) - mid.astype(F32)
    return hi, mid, low.astype(BF16)


def dot_exact_right(a, b, dims=NN):
    hi, lo = split2(a)
    return dot(hi, b, dims) + dot(lo, b, dims)


def dot_exact_left3(a, b):
    hi, mid, low = split3(b)
    return (dot(a, low) + dot(a, mid)) + dot(a, hi)


def wide_dot(a, b, dims=NN):
    ka, kb = dims[0][0][0], dims[0][1][0]
    ah, al = split2(a)
    bh, bl = split2(b)
    return dot(
        jnp.concatenate([ah, al, ah], axis=ka), jnp.concatenate([bh, bh, bl], axis=kb), dims
    )


def three_dots(a, b, dims=NN):
    ah, al = split2(a)
    bh, bl = split2(b)
    return (dot(al, bh, dims) + dot(ah, bl, dims)) + dot(ah, bh, dims)


def iota(shape, dim):
    return lax.broadcasted_iota(jnp.int32, shape, dim)


def head_rows():
    return ((iota((H, D), 1) >> 6) == iota((H, D), 0)).astype(F32).astype(BF16)


def head_columns():
    return ((iota((D, H), 0) >> 6) == iota((D, H), 1)).astype(F32).astype(BF16)


def lower_ones():
    return (iota((L, L), 0) >= iota((L, L), 1)).astype(F32).astype(BF16)


def upper_ones():
    return (iota((L, L), 0) <= iota((L, L), 1)).astype(F32).astype(BF16)


def softplus(v):
    return jnp.maximum(v, 0.0) + jnp.log1p(jnp.exp(-jnp.abs(v)))


def sigmoid(v):
    e = jnp.exp(-jnp.abs(v))
    return jnp.where(v >= 0, 1.0, e) / (1.0 + e)


def pack_payload(pay_ref, state, keep):
    for rg in range(8):
        for lg in range(4):
            lanes = slice(256 * lg, 256 * lg + 256)
            pay_ref[rg * 4 + lg, 0:8, :] = state[8 * rg:8 * rg + 8, lanes]
            pay_ref[rg * 4 + lg, 8:16, :] = jnp.broadcast_to(keep[:, lanes], (8, 256))


def unpack_state(ref, state_ref):
    for rg in range(8):
        for lg in range(4):
            state_ref[8 * rg:8 * rg + 8, 256 * lg:256 * lg + 256] = ref[rg * 4 + lg]


def to_peer(src, dst, send_sem, recv_sem, peer):
    return pltpu.make_async_remote_copy(
        src_ref=src, dst_ref=dst, send_sem=send_sem, recv_sem=recv_sem,
        device_id=peer, device_id_type=MESH,
    )


def places():
    z = lax.axis_index("dp")
    me = lax.axis_index("seq")
    return z, me // 8, lax.rem(me // 2, 4), lax.rem(me, 2)


def greet():
    z = lax.axis_index("dp")
    me = lax.axis_index("seq")
    barrier = pltpu.get_barrier_semaphore()

    def hello(k, _):
        pl.semaphore_signal(
            barrier, inc=1, device_id=(z, lax.rem(me + k, NSEQ)), device_id_type=MESH
        )
        return 0

    def hello_z(k, _):
        pl.semaphore_signal(
            barrier, inc=1, device_id=(lax.rem(z + k, NDP), me), device_id_type=MESH
        )
        return 0

    lax.fori_loop(1, NSEQ, hello, 0)
    lax.fori_loop(1, NDP, hello_z, 0)


def greeted():
    pl.semaphore_wait(pltpu.get_barrier_semaphore(), NSEQ - 1 + NDP - 1)


class Exchange:
    def __init__(self, send, recv, sems):
        self.send, self.recv = send, recv
        self.ss, self.rs = sems.at[0], sems.at[1]

    def start(self):
        z = lax.axis_index("dp")
        me = lax.axis_index("seq")

        def go(k, _):
            to = lax.rem(me + k, NSEQ)
            to_peer(self.send.at[to], self.recv.at[me], self.ss, self.rs, (z, to)).start()
            return 0

        lax.fori_loop(1, NSEQ, go, 0)

    def wait(self):
        z = lax.axis_index("dp")
        me = lax.axis_index("seq")
        most = pl.ds(0, NSEQ - 1)
        copy = to_peer(self.send.at[most], self.recv.at[most], self.ss, self.rs,
                       (z, lax.rem(me + 1, NSEQ)))
        copy.wait_send()
        copy.wait_recv()


def narrow(total):
    return total.astype(BF16)


def narrow_pairs(total):
    start = total.shape[1] - 128
    tail = total[:, start:]
    high = tail.astype(BF16).astype(F32)
    rest = (tail - high)[:, 0:H]
    moved = jnp.concatenate(
        [jnp.zeros_like(rest), rest, jnp.zeros((rest.shape[0], 128 - 2 * H), F32)], axis=1
    )
    lane = iota(tail.shape, 1)
    tail = jnp.where(lane < H, high, tail + moved)
    return jnp.concatenate([total[:, 0:start], tail], axis=1).astype(BF16)


class PlaneSum:
    def __init__(self, part, ra, t, rb, h, rc, sems, x_first, form):
        self.part, self.ra, self.t, self.rb, self.h, self.rc = part, ra, t, rb, h, rc
        self.sems, self.form = sems, form
        z, y, x, core = places()
        self.core = core
        at_x = lambda k: (z, 8 * y + 2 * lax.rem(x + k, 4) + core)
        at_y = lambda k: (z, 8 * lax.rem(y + k, 4) + 2 * x + core)
        self.first = (x, at_x) if x_first else (y, at_y)
        self.second = (y, at_y) if x_first else (x, at_x)
        partner = (z, 8 * y + 2 * x + 1 - core)
        self.pair = to_peer(part.at[1 - core], ra, sems.at[0], sems.at[1], partner)

    def hop(self, src, dst, where, sem):
        here, place = where
        for k in (1, 2, 3):
            to_peer(src.at[lax.rem(here + k, 4)], dst.at[here],
                    self.sems.at[sem], self.sems.at[sem + 1], place(k)).start()

    def hopped(self, src, dst, where, sem):
        here, place = where
        most = pl.ds(0, 3)
        copy = to_peer(src.at[most], dst.at[most], self.sems.at[sem], self.sems.at[sem + 1],
                       place(1))
        copy.wait_send()
        copy.wait_recv()

    def start_pair(self):
        self.pair.start()

    def start_first(self):
        self.pair.wait()

        def body(i, _):
            a, b = i // 4, lax.rem(i, 4)
            self.t[a, b] = self.form(
                self.part[self.core, a, b].astype(F32) + self.ra[a, b].astype(F32)
            )
            return 0

        lax.fori_loop(0, 16, body, 0)
        self.hop(self.t, self.rb, self.first, 2)

    def start_second(self):
        self.hopped(self.t, self.rb, self.first, 2)
        here = self.first[0]

        def body(b, _):
            total = self.t[here, b].astype(F32)
            for k in (1, 2, 3):
                total = total + self.rb[lax.rem(here + k, 4), b].astype(F32)
            self.h[b] = self.form(total)
            return 0

        lax.fori_loop(0, 4, body, 0)
        self.hop(self.h, self.rc, self.second, 4)

    def finish(self):
        self.hopped(self.h, self.rc, self.second, 4)
        here = self.second[0]
        total = self.h[here].astype(F32)
        for k in (1, 2, 3):
            total = total + self.rc[lax.rem(here + k, 4)].astype(F32)
        return total


class DepthSum:
    def __init__(self, zs, zr, zo, sems):
        self.zs, self.zr, self.zo, self.sems = zs, zr, zo, sems
        self.z = lax.axis_index("dp")
        self.me = lax.axis_index("seq")

    def out(self, source, target, sem):
        def go(k, _):
            to = lax.rem(self.z + k, NDP)
            to_peer(source(to), target, self.sems.at[sem], self.sems.at[sem + 1],
                    (to, self.me)).start()
            return 0

        lax.fori_loop(1, NDP, go, 0)

    def done(self, src, dst, sem):
        most = pl.ds(0, NDP - 1)
        copy = to_peer(src.at[most], dst.at[most], self.sems.at[sem], self.sems.at[sem + 1],
                       (lax.rem(self.z + 1, NDP), self.me))
        copy.wait_send()
        copy.wait_recv()

    def start(self):
        self.out(lambda to: self.zs.at[to], self.zr.at[self.z], 0)

    def spread(self):
        self.done(self.zs, self.zr, 0)

        def add(k, total):
            return total + self.zr[lax.rem(self.z + k, NDP)]

        total = lax.fori_loop(1, NDP, add, self.zs[self.z])
        self.zo[self.z] = total * ((NDP * NSEQ * T) ** (-0.5))
        self.out(lambda to: self.zo.at[self.z], self.zo.at[self.z], 2)

    def finish(self):
        self.done(self.zo, self.zo, 2)


def relay_prefix(recv, mid, reverse):
    def step(i, state):
        j = NSEQ - 1 - i if reverse else i
        mid[j] = state
        return recv[j, 8:16] * state + recv[j, 0:8]

    lax.fori_loop(0, NSEQ, step, jnp.zeros((8, 256), F32))


def chunk_rows(c):
    return pl.ds(pl.multiple_of(c * L, L), L)


def keep_row(last, heads):
    return dot_exact_right(jnp.broadcast_to(jnp.exp(last), (8, H)), heads)[0:1]


def keep_row3(total, heads):
    hi, mid, low = split3(jnp.broadcast_to(jnp.exp(total), (8, H)))
    return ((dot(low, heads) + dot(mid, heads)) + dot(hi, heads))[0:1]


def whole_kernel(
    src_ref, dst_ref, isrc_ref, idst_ref, tok_hbm, grad_hbm, wp_hbm, wd_hbm, wo_hbm,
    bias_ref, rate_ref, skip_ref, gain_ref,
    out_ref, gp_out, gd_out, go_out,
    tok, grd, wp, wd, wo, send_t, send_g, recv_t, recv_g, x_ref, g_ref,
    v_ref, bc_ref, raw_ref, run_ref, runt_ref, u_ref, sc_ref, wid_ref, fade_ref,
    pay1, got1, mid1, ent1, pay2, got2, mid2, ent2,
    yin_ref, gn_ref, dy_ref, low_ref, q_ref, dc_ref, db_ref, s_ref, r_ref,
    state_ref, gp_ref, gd_ref, ret, back,
    pa, ra_a, ta, rb_a, ha, rc_a, pb, ra_b, tb, rb_b, hb, rc_b, pw, ra_w, tw, rb_w, hw, rc_w,
    zs1, zr1, zo1, zs2, zr2, zo2,
    load_sems, st_sems, sg_sems, r1_sems, r2_sems, r3_sems, r4_sems, lv_sems,
    a_sems, b_sems, w_sems, z1_sems, z2_sems,
):
    me = lax.axis_index("seq")
    loads = [
        pltpu.make_async_copy(a, b, load_sems.at[i])
        for i, (a, b) in enumerate(
            [(tok_hbm, tok), (grad_hbm, grd), (wp_hbm, wp), (wd_hbm, wd), (wo_hbm, wo)]
        )
    ]
    for load in loads:
        load.start()
    greet()
    tokens_in = Exchange(send_t, recv_t, st_sems)
    grads_in = Exchange(send_g, recv_g, sg_sems)
    loads[0].wait()

    def load_t(d, _):
        send_t[d] = tok[src_ref[0, d]]
        return 0

    def load_g(d, _):
        send_g[d] = grd[src_ref[0, d]]
        return 0

    lax.fori_loop(0, NSEQ, load_t, 0)
    greeted()
    tokens_in.start()
    loads[1].wait()
    lax.fori_loop(0, NSEQ, load_g, 0)
    grads_in.start()
    recv_t[me] = send_t[me]
    recv_g[me] = send_g[me]

    heads = head_rows()
    cols = head_columns()
    lower = lower_ones()
    upper = upper_ones()
    even = iota((1, 128), 1) < 64
    bias = bias_ref[...]
    rate = rate_ref[...]
    gain = gain_ref[...]
    skip = dot_exact_right(jnp.broadcast_to(skip_ref[...], (8, H)), heads)[0:1]
    loads[2].wait()
    loads[3].wait()
    loads[4].wait()
    tokens_in.wait()

    def settle_t(j, _):
        x_ref[pl.ds(pl.multiple_of(j * BLK, BLK), BLK), :] = recv_t[dst_ref[0, j]]
        return 0

    lax.fori_loop(0, NSEQ, settle_t, 0)

    def project(c, carry):
        state, total = carry
        rows = chunk_rows(c)
        x = x_ref[rows, :]
        v = dot(x, wp[:, 0:D])
        v_ref[rows, :] = v
        bc = dot(x, wp[:, D:PROJ])
        bc_ref[rows, :] = bc
        raw = dot(x, wd[...], NT) + bias
        raw_ref[rows, :] = raw
        delta = softplus(raw)
        running = dot_exact_left3(lower, -rate * delta)
        run_ref[rows, :] = running
        runt_ref[c] = running.T
        last = running[L - 1:L, :]
        widened = dot_exact_right(delta, heads)
        wid_ref[rows, :] = widened
        scaled = v * widened
        sc_ref[rows, :] = scaled
        fade = dot_exact_right(jnp.exp(last - running), heads)
        fade_ref[rows, :] = fade
        added = wide_dot(bc[:, 0:N], scaled * fade, TN)
        u_ref[c] = added
        return keep_row(last, heads) * state + added, total + last

    state, total = lax.fori_loop(
        0, NC, project, (jnp.zeros((N, D), F32), jnp.zeros((1, H), F32))
    )
    keep_all = keep_row3(total, heads)
    pack_payload(pay1, state, keep_all)
    ahead = Exchange(pay1, got1, r1_sems)
    ahead.start()
    got1[me] = pay1[me]

    below = iota((L, L), 0) >= iota((L, L), 1)

    def inside_forward(c, _):
        rows = chunk_rows(c)
        bc = bc_ref[rows, :]
        running = run_ref[rows, :]
        runt = runt_ref[c]
        scores = wide_dot(bc[:, N:2 * N], bc[:, 0:N], NT)
        scaled = sc_ref[rows, :].astype(BF16)
        for j in range(H // 2):
            mixes = []
            for h in (2 * j, 2 * j + 1):
                spread = running[:, h:h + 1] - runt[h:h + 1, :]
                decay = jnp.exp(jnp.where(below, spread, -jnp.inf))
                mixes.append((decay * scores).astype(BF16))
            pair = scaled[:, 128 * j:128 * j + 128]
            zero = jnp.zeros_like(pair)
            stacked = jnp.concatenate(
                [jnp.where(even, pair, zero), jnp.where(even, zero, pair)], axis=0
            )
            yin_ref[rows, 128 * j:128 * j + 128] = dot(jnp.concatenate(mixes, axis=1), stacked)
        return 0

    lax.fori_loop(0, 2, inside_forward, 0)
    ahead.wait()
    relay_prefix(got1, mid1, False)
    ahead_back = Exchange(mid1, ent1, r2_sems)
    ahead_back.start()
    ent1[me] = mid1[me]
    lax.fori_loop(2, NC, inside_forward, 0)
    grads_in.wait()

    def settle_g(j, _):
        g_ref[pl.ds(pl.multiple_of(j * BLK, BLK), BLK), :] = recv_g[dst_ref[0, j]]
        return 0

    lax.fori_loop(0, NSEQ, settle_g, 0)

    def project_grads(c, _):
        rows = chunk_rows(c)
        gn_ref[rows, :] = dot(g_ref[rows, :], wo[...], NT) * gain
        return 0

    lax.fori_loop(0, NC, project_grads, 0)
    ahead_back.wait()
    unpack_state(ent1, state_ref)

    def forward(c, carry):
        out_grad, before = carry
        rows = chunk_rows(c)
        r = bc_ref[rows, N:2 * N]
        running = run_ref[rows, :]
        last = running[L - 1:L, :]
        state = state_ref[...]
        s_ref[c] = state
        grown = dot_exact_right(jnp.exp(running), heads)
        carried = wide_dot(r, state) * grown
        summed = yin_ref[rows, :] + carried + skip * v_ref[rows, :]
        square = dot_exact_right(summed * summed, cols) * (1.0 / P_SIZE)
        scale = dot_exact_right(lax.rsqrt(square + EPSILON), heads)
        unit = summed * scale
        low_ref[rows, :] = (unit * gain).astype(BF16)
        grad_unit = gn_ref[rows, :]
        along = dot_exact_right(grad_unit * unit, cols) * (1.0 / P_SIZE)
        dy = scale * (grad_unit - unit * dot_exact_right(along, heads))
        dy_ref[rows, :] = dy
        q_ref[rows, :] = dot_exact_right(dy * carried, cols)
        back_in = dy * grown
        dc_ref[rows, :] = three_dots(back_in, state, NT)
        reach = wide_dot(r, back_in, TN)
        r_ref[c] = reach
        keep = keep_row(last, heads)
        state_ref[...] = keep * state + u_ref[c]
        return out_grad + before * reach, before * keep

    out_grad, _ = lax.fori_loop(
        0, NC, forward, (jnp.zeros((N, D), F32), jnp.ones((1, D), F32))
    )
    pack_payload(pay2, out_grad, keep_all)
    astern = Exchange(pay2, got2, r3_sems)
    astern.start()
    got2[me] = pay2[me]

    sum_a = PlaneSum(pa, ra_a, ta, rb_a, ha, rc_a, a_sems, True, narrow)
    sum_b = PlaneSum(pb, ra_b, tb, rb_b, hb, rc_b, b_sems, False, narrow_pairs)
    sum_w = PlaneSum(pw, ra_w, tw, rb_w, hw, rc_w, w_sems, True, narrow)
    deep1 = DepthSum(zs1, zr1, zo1, z1_sems)
    deep2 = DepthSum(zs2, zr2, zo2, z2_sems)

    def spots(m):
        for k in range(4):
            d = 4 * m + k
            yield d >> 3, (d >> 1) & 3, d & 1, slice(32 * k, 32 * k + 32)

    low = low_ref[...]
    for m in range(8):
        gt = g_ref[:, 128 * m:128 * m + 128].T
        out_rows = dot(gt, low).astype(BF16)
        for y, x, core, sub in spots(m):
            pw[core, x, y] = out_rows[sub]
    sum_w.start_pair()
    astern.wait()
    relay_prefix(got2, mid2, True)
    astern_back = Exchange(mid2, ent2, r4_sems)
    astern_back.start()
    ent2[me] = mid2[me]
    sum_w.start_first()

    after = iota((L, L), 1) >= iota((L, L), 0)
    half = iota((2 * L, H), 0) >> 7
    pick = iota((2 * L, H), 1)
    halft = iota((H, 2 * L), 1) >> 7
    pickt = iota((H, 2 * L), 0)

    def inside_backward(c, _):
        rows = chunk_rows(c)
        bc = bc_ref[rows, :]
        b, r = bc[:, 0:N], bc[:, N:2 * N]
        running = run_ref[rows, :]
        runt = runt_ref[c]
        dy_low = dy_ref[rows, :].astype(BF16)
        scaled = sc_ref[rows, :].astype(BF16)
        scores_t = wide_dot(b, r, NT)
        dscores_t = jnp.zeros((L, L), F32)
        by_source = jnp.zeros((L, H), F32)
        by_target = jnp.zeros((H, L), F32)
        for j in range(H // 2):
            pair = slice(128 * j, 128 * j + 128)
            sp = scaled[:, pair]
            dp = dy_low[:, pair]
            zero = jnp.zeros_like(sp)
            mixes, flows = [], []
            for e in (0, 1):
                h = 2 * j + e
                spread = runt[h:h + 1, :] - running[:, h:h + 1]
                decay = jnp.exp(jnp.where(after, spread, -jnp.inf))
                mixes.append((decay * scores_t).astype(BF16))
                mine = jnp.where(even, sp, zero) if e == 0 else jnp.where(even, zero, sp)
                moved = dot(mine, dp, NT) * decay
                dscores_t = dscores_t + moved
                flows.append((moved * scores_t).astype(BF16))
            stacked = jnp.concatenate(
                [jnp.where(even, dp, zero), jnp.where(even, zero, dp)], axis=0
            )
            yin_ref[rows, pair] = dot(jnp.concatenate(mixes, axis=1), stacked)
            which = (pick == 2 * j + half).astype(F32).astype(BF16)
            which_t = (pickt == 2 * j + halft).astype(F32).astype(BF16)
            by_source = by_source + dot(jnp.concatenate(flows, axis=1), which)
            by_target = by_target + dot(which_t, jnp.concatenate(flows, axis=0))
        db_ref[rows, :] = three_dots(dscores_t, r)
        dc_ref[rows, :] = dc_ref[rows, :] + three_dots(dscores_t, b, TN)
        q_ref[rows, :] = q_ref[rows, :] + (by_target.T - by_source)
        return 0

    lax.fori_loop(0, 2, inside_backward, 0)
    sum_w.start_second()
    lax.fori_loop(2, NC, inside_backward, 0)
    sum_rows = sum_w.finish()
    for i in range(4):
        for k in range(2):
            zs2[4 * k + i] = sum_rows[8 * i:8 * i + 8, 512 * k:512 * k + 512]
    deep2.start()
    astern_back.wait()
    unpack_state(ent2, state_ref)

    def backward(i, _):
        c = NC - 1 - i
        rows = chunk_rows(c)
        bc = bc_ref[rows, :]
        b = bc[:, 0:N]
        running = run_ref[rows, :]
        last = running[L - 1:L, :]
        grad = state_ref[...]
        fade = fade_ref[rows, :]
        weighted = sc_ref[rows, :] * fade
        d_weighted = wide_dot(b, grad)
        used = dot_exact_right(d_weighted * weighted, cols)
        db = db_ref[rows, :] + three_dots(weighted, grad, NT)
        keep = keep_row(last, heads)
        held = jnp.sum(keep * grad * s_ref[c], axis=0, keepdims=True)
        held = dot_exact_right(jnp.broadcast_to(held, (8, D)), cols)[0:1]
        d_scaled = d_weighted * fade + yin_ref[rows, :]
        d_running = q_ref[rows, :] - used
        d_last = jnp.sum(used, axis=0, keepdims=True) + held
        d_decay = dot_exact_left3(upper, d_running) + d_last
        d_delta = dot_exact_right(d_scaled * v_ref[rows, :], cols) - rate * d_decay
        gd = (d_delta * sigmoid(raw_ref[rows, :])).astype(BF16)
        gd_ref[rows, :] = gd
        gp_ref[rows, 0:D] = (d_scaled * wid_ref[rows, :] + skip * dy_ref[rows, :]).astype(BF16)
        gp_ref[rows, D:PROJ] = jnp.concatenate([db, dc_ref[rows, :]], axis=1).astype(BF16)
        state_ref[...] = r_ref[c] + keep * grad
        gs = dot(gp_ref[rows, :], wp[...], NT) + dot(gd, wd[...])
        tok[pl.ds(c * (L // BLK), L // BLK)] = gs.astype(BF16).reshape(L // BLK, BLK, D)
        return 0

    lax.fori_loop(0, NC, backward, 0)

    def send_back(d, _):
        ret[d] = tok[idst_ref[0, d]]
        return 0

    lax.fori_loop(0, NSEQ, send_back, 0)
    grads_back = Exchange(ret, back, lv_sems)
    grads_back.start()
    back[me] = ret[me]
    deep2.spread()

    gp = gp_ref[...]
    gd = gd_ref[...]
    for m in range(8):
        xt = x_ref[:, 128 * m:128 * m + 128].T
        rows_p = dot(xt, gp)
        rows_d = dot(xt, gd)
        dt_hi, dt_lo = split2(rows_d)
        rows_p = rows_p.astype(BF16)
        rows_d = jnp.concatenate([dt_hi, dt_lo, jnp.zeros((128, 128 - 2 * H), BF16)], axis=1)
        for y, x, core, sub in spots(m):
            pa[core, x, y] = rows_p[sub, 0:HALF]
            pb[core, y, x, :, 0:PROJ - HALF] = rows_p[sub, HALF:PROJ]
            pb[core, y, x, :, PROJ - HALF:HALF] = rows_d[sub]
    sum_a.start_pair()
    sum_b.start_pair()
    sum_a.start_first()
    sum_b.start_first()
    sum_a.start_second()
    sum_b.start_second()
    for k, plane in enumerate((sum_a, sum_b)):
        sum_rows = plane.finish()
        for i in range(4):
            zs1[4 * k + i] = sum_rows[8 * i:8 * i + 8]
    deep1.start()
    grads_back.wait()

    def settle_back(j, _):
        out_ref[j] = back[isrc_ref[0, j]]
        return 0

    lax.fori_loop(0, NSEQ, settle_back, 0)
    deep2.finish()
    for i in range(4):
        for k in range(2):
            go_out[8 * i:8 * i + 8, 512 * k:512 * k + 512] = zo2[4 * k + i]
    deep1.spread()
    deep1.finish()
    for i in range(4):
        rows = slice(8 * i, 8 * i + 8)
        gp_out[rows, 0:HALF] = zo1[i]
        gp_out[rows, HALF:PROJ] = zo1[4 + i, :, 0:PROJ - HALF]
        gd_out[rows, :] = zo1[4 + i, :, PROJ - HALF:HALF]


def local(tokens, grad_out, src_order, dst_order, w_proj, w_dt, w_out,
          dt_bias, decay_rate, d_skip, norm_gain):
    blocks = (NSEQ, BLK, D)
    vm = pltpu.VMEM
    dma = pltpu.SemaphoreType.DMA
    block = vm(blocks, BF16)
    full = vm((T, D), F32)
    low = vm((T, D), BF16)
    states = vm((NC, N, D), F32)
    pay, piece = vm((NSEQ, 16, 256), F32), vm((NSEQ, 8, 256), F32)

    def plane(width):
        line = vm((4, 32, width), BF16)
        square = vm((4, 4, 32, width), BF16)
        return [vm((2, 4, 4, 32, width), BF16), square, square, square, line, line]

    scratch = (
        [block, block, vm((D, PROJ), BF16), vm((H, D), BF16), vm((D, D), BF16)]
        + [block] * 4 + [low] * 2
        + [full, vm((T, 2 * N), F32), vm((T, H), F32), vm((T, H), F32), vm((NC, H, L), F32)]
        + [states] + [full] * 3
        + [pay, pay, piece, piece] * 2
        + [full, full, full, low, vm((T, H), F32), vm((T, N), F32), vm((T, N), F32)]
        + [states, states]
        + [vm((N, D), F32), vm((T, PROJ), BF16), vm((T, H), BF16), block, block]
        + plane(HALF) + plane(HALF) + plane(D)
        + [vm((NDP, 8, HALF), F32)] * 3 + [vm((NDP, 8, 512), F32)] * 3
        + [dma((5,))] + [dma((2,))] * 7 + [dma((6,))] * 3 + [dma((4,))] * 2
    )
    order = jnp.arange(NSEQ, dtype=jnp.int32)

    def inverse(perm):
        return jnp.sum(
            jnp.where(perm[0][None, :] == order[:, None], order[None, :], 0), axis=1,
            dtype=jnp.int32,
        ).reshape(1, NSEQ)

    hbm = pl.BlockSpec(memory_space=pl.ANY)
    grad_tokens, gp, gd, go = pl.pallas_call(
        whole_kernel,
        out_shape=[
            jax.ShapeDtypeStruct(blocks, BF16),
            jax.ShapeDtypeStruct((32, PROJ), F32),
            jax.ShapeDtypeStruct((32, 128), F32),
            jax.ShapeDtypeStruct((32, D), F32),
        ],
        in_specs=[SM] * 4 + [hbm] * 5 + [VM] * 4,
        out_specs=[VM] * 4,
        scratch_shapes=scratch,
        compiler_params=pltpu.CompilerParams(
            collective_id=0, has_side_effects=True, vmem_limit_bytes=VMEM_LIMIT
        ),
        name="whole",
    )(
        src_order, dst_order, inverse(src_order), inverse(dst_order),
        tokens.reshape(blocks), grad_out.reshape(blocks), w_proj, w_dt.T, w_out,
        dt_bias.reshape(1, H), decay_rate.reshape(1, H), d_skip.reshape(1, H),
        norm_gain.reshape(1, D),
    )
    return grad_tokens.reshape(1, T, D), gp, gd[:, 0:H] + gd[:, H:2 * H], go.T


def solution(mesh):
    in_specs = (
        P("dp", "seq", None), P("dp", "seq", None), P("seq", None), P("seq", None),
        P(), P(), P(), P(), P(), P(), P(),
    )
    out_specs = (P("dp", "seq", None), P("seq", None), P("seq", None), P(None, "seq"))
    return jax.shard_map(local, mesh=mesh, in_specs=in_specs, out_specs=out_specs, check_vma=False)
```

time: 1550 us -> 147 us (0.09)
  waiting for transfers between devices: 834 us -> 0 us
  starting transfers between devices: 257 us -> 0 us
  Pallas kernels: 0 us -> 138 us
  local copies, waits for them, and re-layouts: 143 us -> 5.17 us
  other arithmetic: 141 us -> 3.43 us
  matrix products: 105 us -> 0 us
  blocking collectives: 40.2 us -> 0 us
    ppermute x62 -> x0, waiting for transfers between devices: 544 us -> none  [passed_along(): return lax.ppermute(value, axis, pairs)]
    ppermute x62 -> x0, starting transfers between devices: 242 us -> none  [passed_along(): return lax.ppermute(value, axis, pairs)]
    reduce_scatter x2 -> x0, waiting for transfers between devices: 170 us -> none  [the longest x1 95.2 us: local(): lax.psum_scatter(column_term(scan_tokens, grad_proj), 'seq', scatter_dime...]
    pallas_call x0 -> x1, Pallas kernels: none -> 138 us  [local(): pl.pallas_call(whole_kernel, out_shape=[jax.ShapeDtypeStruct(blocks, BF16...]
    dot_general x37 -> x0, matrix products: 104 us -> none  [the longest x6 38.3 us: span_step(): inside = jnp.einsum('hts,shp->thp', mixing, values, precision=HIGHEST)]
    psum x1 -> x0, waiting for transfers between devices: 71.3 us -> none  [local(): lax.psum((proj_part, out_part, delta_part), 'dp')]
    add x64 -> x1, other arithmetic: 68.3 us -> 0.87 us  [local(): return (grad_tokens.reshape(1, T, D), gp, gd[:, 0:H] + gd[:, H:2 * H], go.T)]
    unnamed x5 -> x0, waiting for transfers between devices: 37.5 us -> none
  transfers between devices with their start and end apart: 68 -> 0, of which waited for: 67 -> 0; matrix products, arithmetic and copies ran while one was open for 4% -> 0% of each run, Pallas kernels for 0% -> 0%
where the time goes in v2:
time: 147 us
  Pallas kernels  138 us (94%)
  local copies, waits for them, and re-layouts  5.17 us (4%)
  other arithmetic  3.43 us (2%)
    pallas_call x1, Pallas kernels, local(): pl.pallas_call(whole_kernel, out_shape=[jax.ShapeDtypeStruct(blocks, BF16...  138 us
    unnamed x6, local copies, waits for them, and re-layouts  5.17 us

profile of v2, /device:TPU:24, one launch (start us, length us, event | category | flops | bytes accessed | tf_op | source)
XLA Modules:
  0.0 147.3 jit_solution(11458249087370004781)
XLA Ops:
  0.6 1.3 select_reduce_fusion
  1.9 1.3 select_reduce_fusion.1
  3.2 138.0 %whole.1 = (bf16[32,16,1024]{2,1,0:T(8,128)(2,1)}, f32[32,1152]{1,0:T(8,128)}, f32[32,128]{1,0:T(8,128)}, f32[32,1024]{1,0:T(8,128)}) custom-call(s32[1,32]{1,0:T(1,128)} %src_ref.1, s32[1,32]{1,0:T(1,128)} %dst_ref.1, s32[1,32]{1,0:T(1,128)} %bitcast.25, s32[1,32]{1,0:T(1,128)} %bitcast.24, bf16[32,16,1024]{2,1,0:T(8,128)(2,1)} %bitcast.14, ...), custom_call_target="tpu_custom_call" | custom-call | tf_op jit(solution)/shard_map/whole/pallas_call | solution.py:715
  141.2 0.0 copy-start
  141.2 0.9 slice_add_fusion
  142.1 0.7 copy.16
  142.8 2.3 %copy.20 = bf16[1,512,1024]{2,1,0:T(8,128)(2,1)} copy(bf16[1,512,1024]{2,1,0:T(8,128)(2,1)} %bitcast.13) | data formatting | bytes 2097152
  145.0 1.6 %copy.21 = f32[32,1152]{1,0:T(8,128)} copy(f32[32,1152]{1,0:T(8,128)} %get-tuple-element.25) | data formatting | bytes 294912
  146.6 0.0 copy-done
  146.6 0.7 copy.22
Async XLA Ops:
  141.2 5.4 %copy-start = (f32[32,1024]{1,0:T(8,128)S(1)}, f32[32,1024]{1,0:T(8,128)}, u32[]{:S(2)}) copy-start(f32[32,1024]{1,0:T(8,128)} %get-tuple-element.11) | copy-start | bytes 393220

commit v3 on v2

--- a/solution.py
+++ b/solution.py
@@ -24,6 +24,8 @@
 MESH = pl.DeviceIdType.MESH
 VMEM_LIMIT = 62 * 1024 * 1024
 HALF = 640
+SPLIT = 13
+UNROLL = 2
 
 VM = pl.BlockSpec(memory_space=pltpu.VMEM)
 SM = pl.BlockSpec(memory_space=pltpu.SMEM)
@@ -73,6 +75,22 @@
     return (dot(al, bh, dims) + dot(ah, bl, dims)) + dot(ah, bh, dims)
 
 
+def expand(a, heads2):
+    return dot(jnp.concatenate(split2(a), axis=1), heads2)
+
+
+def thrice(a, axis, second):
+    hi, lo = split2(a)
+    return jnp.concatenate([hi, hi, lo] if second else [hi, lo, hi], axis=axis)
+
+
+def head_means(a, block):
+    low = a.astype(BF16)
+    return jnp.concatenate(
+        [dot(low[:, 128 * j:128 * j + 128], block) for j in range(8)], axis=1
+    ) * (1.0 / P_SIZE)
+
+
 def iota(shape, dim):
     return lax.broadcasted_iota(jnp.int32, shape, dim)
 
@@ -102,12 +120,16 @@
     return jnp.where(v >= 0, 1.0, e) / (1.0 + e)
 
 
-def pack_payload(pay_ref, state, keep):
+def pack_payload(pay_ref, state_ref, keep=None):
     for rg in range(8):
         for lg in range(4):
             lanes = slice(256 * lg, 256 * lg + 256)
-            pay_ref[rg * 4 + lg, 0:8, :] = state[8 * rg:8 * rg + 8, lanes]
-            pay_ref[rg * 4 + lg, 8:16, :] = jnp.broadcast_to(keep[:, lanes], (8, 256))
+            pay_ref[rg * 4 + lg, :, 0:256] = state_ref[8 * rg:8 * rg + 8, lanes]
+            if keep is not None:
+                first = keep[:, 256 * lg:256 * lg + 128]
+                second = keep[:, 256 * lg + 128:256 * lg + 256]
+                row = iota((8, 128), 0)
+                pay_ref[rg * 4 + lg, :, 256:384] = jnp.where(row == 0, first, second)
 
 
 def unpack_state(ref, state_ref):
@@ -146,8 +168,10 @@
         )
         return 0
 
-    lax.fori_loop(1, NSEQ, hello, 0)
-    lax.fori_loop(1, NDP, hello_z, 0)
+    for k in range(1, NSEQ):
+        hello(k, 0)
+    for k in range(1, NDP):
+        hello_z(k, 0)
 
 
 def greeted():
@@ -159,16 +183,12 @@
         self.send, self.recv = send, recv
         self.ss, self.rs = sems.at[0], sems.at[1]
 
-    def start(self):
+    def start(self, first=1, last=NSEQ):
         z = lax.axis_index("dp")
         me = lax.axis_index("seq")
-
-        def go(k, _):
+        for k in range(first, last):
             to = lax.rem(me + k, NSEQ)
             to_peer(self.send.at[to], self.recv.at[me], self.ss, self.rs, (z, to)).start()
-            return 0
-
-        lax.fori_loop(1, NSEQ, go, 0)
 
     def wait(self):
         z = lax.axis_index("dp")
@@ -270,13 +290,10 @@
         self.me = lax.axis_index("seq")
 
     def out(self, source, target, sem):
-        def go(k, _):
+        for k in range(1, NDP):
             to = lax.rem(self.z + k, NDP)
             to_peer(source(to), target, self.sems.at[sem], self.sems.at[sem + 1],
                     (to, self.me)).start()
-            return 0
-
-        lax.fori_loop(1, NDP, go, 0)
 
     def done(self, src, dst, sem):
         most = pl.ds(0, NDP - 1)
@@ -291,10 +308,9 @@
     def spread(self):
         self.done(self.zs, self.zr, 0)
 
-        def add(k, total):
-            return total + self.zr[lax.rem(self.z + k, NDP)]
-
-        total = lax.fori_loop(1, NDP, add, self.zs[self.z])
+        total = self.zs[self.z]
+        for k in range(1, NDP):
+            total = total + self.zr[lax.rem(self.z + k, NDP)]
         self.zo[self.z] = total * ((NDP * NSEQ * T) ** (-0.5))
         self.out(lambda to: self.zo.at[self.z], self.zo.at[self.z], 2)
 
@@ -302,13 +318,14 @@
         self.done(self.zo, self.zo, 2)
 
 
-def relay_prefix(recv, mid, reverse):
+def relay_prefix(recv, mid, keeps, reverse):
     def step(i, state):
         j = NSEQ - 1 - i if reverse else i
         mid[j] = state
-        return recv[j, 8:16] * state + recv[j, 0:8]
-
-    lax.fori_loop(0, NSEQ, step, jnp.zeros((8, 256), F32))
+        keep = jnp.concatenate([keeps[j, 0:1, 256:384], keeps[j, 1:2, 256:384]], axis=1)
+        return keep * state + recv[j, :, 0:256]
+
+    lax.fori_loop(0, NSEQ, step, jnp.zeros((8, 256), F32), unroll=4)
 
 
 def chunk_rows(c):
@@ -325,18 +342,19 @@
 
 
 def whole_kernel(
-    src_ref, dst_ref, isrc_ref, idst_ref, tok_hbm, grad_hbm, wp_hbm, wd_hbm, wo_hbm,
+    src_ref, dst_ref, tok_hbm, grad_hbm, wp_hbm, wd_hbm, wo_hbm,
     bias_ref, rate_ref, skip_ref, gain_ref,
-    out_ref, gp_out, gd_out, go_out,
-    tok, grd, wp, wd, wo, send_t, send_g, recv_t, recv_g, x_ref, g_ref,
+    back, zo1, zo2,
+    tok, grd, wp, wd, wo, wpt, wot, xt_ref, send_t, send_g, recv_t, recv_g, x_ref, g_ref,
     v_ref, bc_ref, raw_ref, run_ref, runt_ref, u_ref, sc_ref, wid_ref, fade_ref,
     pay1, got1, mid1, ent1, pay2, got2, mid2, ent2,
     yin_ref, gn_ref, dy_ref, low_ref, q_ref, dc_ref, db_ref, s_ref, r_ref,
-    state_ref, gp_ref, gd_ref, ret, back,
-    pa, ra_a, ta, rb_a, ha, rc_a, pb, ra_b, tb, rb_b, hb, rc_b, pw, ra_w, tw, rb_w, hw, rc_w,
-    zs1, zr1, zo1, zs2, zr2, zo2,
+    state_ref, keep_ref, gp_ref, gd_ref, ret, inv_ref,
+    pa, ra_a, ta, rb_a, ha, rc_a, pb, ra_b, tb, rb_b, hb, rc_b,
+    pv, ra_v, tv, rb_v, hv, rc_v, pw, ra_w, tw, rb_w, hw, rc_w,
+    zs1, zr1, zs2, zr2,
     load_sems, st_sems, sg_sems, r1_sems, r2_sems, r3_sems, r4_sems, lv_sems,
-    a_sems, b_sems, w_sems, z1_sems, z2_sems,
+    a_sems, b_sems, v_sems, w_sems, z1_sems, z2_sems,
 ):
     me = lax.axis_index("seq")
     loads = [
@@ -345,9 +363,9 @@
             [(tok_hbm, tok), (grad_hbm, grd), (wp_hbm, wp), (wd_hbm, wd), (wo_hbm, wo)]
         )
     ]
-    for load in loads:
-        load.start()
+    loads[0].start()
     greet()
+    loads[1].start()
     tokens_in = Exchange(send_t, recv_t, st_sems)
     grads_in = Exchange(send_g, recv_g, sg_sems)
     loads[0].wait()
@@ -360,12 +378,22 @@
         send_g[d] = grd[src_ref[0, d]]
         return 0
 
-    lax.fori_loop(0, NSEQ, load_t, 0)
+    def invert(s, _):
+        place = 0
+        for j in range(NSEQ):
+            place = jnp.where(dst_ref[0, j] == s, j, place)
+        inv_ref[0, s] = place
+        return 0
+
+    lax.fori_loop(0, NSEQ, load_t, 0, unroll=4)
+    loads[1].wait()
+    lax.fori_loop(0, NSEQ, load_g, 0, unroll=4)
+    for load in loads[2:]:
+        load.start()
+    lax.fori_loop(0, NSEQ, invert, 0)
     greeted()
     tokens_in.start()
-    loads[1].wait()
-    lax.fori_loop(0, NSEQ, load_g, 0)
-    grads_in.start()
+    grads_in.start(1, SPLIT)
     recv_t[me] = send_t[me]
     recv_g[me] = send_g[me]
 
@@ -374,6 +402,8 @@
     lower = lower_ones()
     upper = upper_ones()
     even = iota((1, 128), 1) < 64
+    heads2 = jnp.concatenate([heads, heads], axis=0)
+    block = ((iota((128, 128), 0) >> 6) == (iota((128, 128), 1) >> 6)).astype(F32).astype(BF16)
     bias = bias_ref[...]
     rate = rate_ref[...]
     gain = gain_ref[...]
@@ -381,16 +411,17 @@
     loads[2].wait()
     loads[3].wait()
     loads[4].wait()
+    wpt[...] = wp[...].T
+    wot[...] = wo[...].T
     tokens_in.wait()
 
     def settle_t(j, _):
         x_ref[pl.ds(pl.multiple_of(j * BLK, BLK), BLK), :] = recv_t[dst_ref[0, j]]
         return 0
 
-    lax.fori_loop(0, NSEQ, settle_t, 0)
-
-    def project(c, carry):
-        state, total = carry
+    lax.fori_loop(0, NSEQ, settle_t, 0, unroll=4)
+
+    def project(c, total):
         rows = chunk_rows(c)
         x = x_ref[rows, :]
         v = dot(x, wp[:, 0:D])
@@ -404,24 +435,27 @@
         run_ref[rows, :] = running
         runt_ref[c] = running.T
         last = running[L - 1:L, :]
-        widened = dot_exact_right(delta, heads)
+        keep_ref[c] = keep_row(last, heads)
+        widened = expand(delta, heads2)
         wid_ref[rows, :] = widened
         scaled = v * widened
         sc_ref[rows, :] = scaled
-        fade = dot_exact_right(jnp.exp(last - running), heads)
+        fade = expand(jnp.exp(last - running), heads2)
         fade_ref[rows, :] = fade
-        added = wide_dot(bc[:, 0:N], scaled * fade, TN)
-        u_ref[c] = added
-        return keep_row(last, heads) * state + added, total + last
-
-    state, total = lax.fori_loop(
-        0, NC, project, (jnp.zeros((N, D), F32), jnp.zeros((1, H), F32))
-    )
+        u_ref[c] = wide_dot(bc[:, 0:N], scaled * fade, TN)
+        return total + last
+
+    total = lax.fori_loop(0, NC, project, jnp.zeros((1, H), F32), unroll=UNROLL)
     keep_all = keep_row3(total, heads)
-    pack_payload(pay1, state, keep_all)
+    state_ref[...] = u_ref[0]
+    for c in range(1, NC):
+        state_ref[...] = keep_ref[c] * state_ref[...] + u_ref[c]
+    pack_payload(pay1, state_ref, keep_all)
     ahead = Exchange(pay1, got1, r1_sems)
     ahead.start()
+    grads_in.start(SPLIT, NSEQ)
     got1[me] = pay1[me]
+    xt_ref[...] = x_ref[...].T
 
     below = iota((L, L), 0) >= iota((L, L), 1)
 
@@ -446,69 +480,64 @@
             yin_ref[rows, 128 * j:128 * j + 128] = dot(jnp.concatenate(mixes, axis=1), stacked)
         return 0
 
-    lax.fori_loop(0, 2, inside_forward, 0)
+    lax.fori_loop(0, 3, inside_forward, 0)
     ahead.wait()
-    relay_prefix(got1, mid1, False)
+    relay_prefix(got1, mid1, got1, False)
     ahead_back = Exchange(mid1, ent1, r2_sems)
     ahead_back.start()
     ent1[me] = mid1[me]
-    lax.fori_loop(2, NC, inside_forward, 0)
+    lax.fori_loop(3, NC, inside_forward, 0)
     grads_in.wait()
 
     def settle_g(j, _):
         g_ref[pl.ds(pl.multiple_of(j * BLK, BLK), BLK), :] = recv_g[dst_ref[0, j]]
         return 0
 
-    lax.fori_loop(0, NSEQ, settle_g, 0)
+    lax.fori_loop(0, NSEQ, settle_g, 0, unroll=4)
 
     def project_grads(c, _):
         rows = chunk_rows(c)
-        gn_ref[rows, :] = dot(g_ref[rows, :], wo[...], NT) * gain
+        gn_ref[rows, :] = dot(g_ref[rows, :], wot[...]) * gain
         return 0
 
     lax.fori_loop(0, NC, project_grads, 0)
     ahead_back.wait()
-    unpack_state(ent1, state_ref)
-
-    def forward(c, carry):
-        out_grad, before = carry
+    unpack_state(ent1, s_ref.at[0])
+    for c in range(1, NC):
+        s_ref[c] = keep_ref[c - 1] * s_ref[c - 1] + u_ref[c - 1]
+
+    def forward(c, _):
         rows = chunk_rows(c)
         r = bc_ref[rows, N:2 * N]
-        running = run_ref[rows, :]
-        last = running[L - 1:L, :]
-        state = state_ref[...]
-        s_ref[c] = state
-        grown = dot_exact_right(jnp.exp(running), heads)
+        state = s_ref[c]
+        grown = expand(jnp.exp(run_ref[rows, :]), heads2)
         carried = wide_dot(r, state) * grown
         summed = yin_ref[rows, :] + carried + skip * v_ref[rows, :]
-        square = dot_exact_right(summed * summed, cols) * (1.0 / P_SIZE)
-        scale = dot_exact_right(lax.rsqrt(square + EPSILON), heads)
+        scale = lax.rsqrt(head_means(summed * summed, block) + EPSILON)
         unit = summed * scale
         low_ref[rows, :] = (unit * gain).astype(BF16)
         grad_unit = gn_ref[rows, :]
-        along = dot_exact_right(grad_unit * unit, cols) * (1.0 / P_SIZE)
-        dy = scale * (grad_unit - unit * dot_exact_right(along, heads))
+        dy = scale * (grad_unit - unit * head_means(grad_unit * unit, block))
         dy_ref[rows, :] = dy
-        q_ref[rows, :] = dot_exact_right(dy * carried, cols)
+        q_ref[rows, :] = dot((dy * carried).astype(BF16), cols)
         back_in = dy * grown
         dc_ref[rows, :] = three_dots(back_in, state, NT)
-        reach = wide_dot(r, back_in, TN)
-        r_ref[c] = reach
-        keep = keep_row(last, heads)
-        state_ref[...] = keep * state + u_ref[c]
-        return out_grad + before * reach, before * keep
-
-    out_grad, _ = lax.fori_loop(
-        0, NC, forward, (jnp.zeros((N, D), F32), jnp.ones((1, D), F32))
-    )
-    pack_payload(pay2, out_grad, keep_all)
+        r_ref[c] = wide_dot(r, back_in, TN)
+        return 0
+
+    lax.fori_loop(0, NC, forward, 0, unroll=UNROLL)
+    state_ref[...] = r_ref[NC - 1]
+    for c in range(NC - 2, -1, -1):
+        state_ref[...] = keep_ref[c] * state_ref[...] + r_ref[c]
+    pack_payload(pay2, state_ref)
     astern = Exchange(pay2, got2, r3_sems)
     astern.start()
     got2[me] = pay2[me]
 
     sum_a = PlaneSum(pa, ra_a, ta, rb_a, ha, rc_a, a_sems, True, narrow)
     sum_b = PlaneSum(pb, ra_b, tb, rb_b, hb, rc_b, b_sems, False, narrow_pairs)
-    sum_w = PlaneSum(pw, ra_w, tw, rb_w, hw, rc_w, w_sems, True, narrow)
+    sum_v = PlaneSum(pv, ra_v, tv, rb_v, hv, rc_v, v_sems, True, narrow)
+    sum_w = PlaneSum(pw, ra_w, tw, rb_w, hw, rc_w, w_sems, False, narrow)
     deep1 = DepthSum(zs1, zr1, zo1, z1_sems)
     deep2 = DepthSum(zs2, zr2, zo2, z2_sems)
 
@@ -522,15 +551,10 @@
         gt = g_ref[:, 128 * m:128 * m + 128].T
         out_rows = dot(gt, low).astype(BF16)
         for y, x, core, sub in spots(m):
-            pw[core, x, y] = out_rows[sub]
+            pv[core, x, y] = out_rows[sub, 0:512]
+            pw[core, y, x] = out_rows[sub, 512:D]
+    sum_v.start_pair()
     sum_w.start_pair()
-    astern.wait()
-    relay_prefix(got2, mid2, True)
-    astern_back = Exchange(mid2, ent2, r4_sems)
-    astern_back.start()
-    ent2[me] = mid2[me]
-    sum_w.start_first()
-
     after = iota((L, L), 1) >= iota((L, L), 0)
     half = iota((2 * L, H), 0) >> 7
     pick = iota((2 * L, H), 1)
@@ -578,62 +602,49 @@
         return 0
 
     lax.fori_loop(0, 2, inside_backward, 0)
+    astern.wait()
+    relay_prefix(got2, mid2, got1, True)
+    astern_back = Exchange(mid2, ent2, r4_sems)
+    astern_back.start()
+    ent2[me] = mid2[me]
+    sum_v.start_first()
+    sum_w.start_first()
+    lax.fori_loop(2, NC, inside_backward, 0)
+    sum_v.start_second()
     sum_w.start_second()
-    lax.fori_loop(2, NC, inside_backward, 0)
-    sum_rows = sum_w.finish()
-    for i in range(4):
-        for k in range(2):
-            zs2[4 * k + i] = sum_rows[8 * i:8 * i + 8, 512 * k:512 * k + 512]
-    deep2.start()
     astern_back.wait()
-    unpack_state(ent2, state_ref)
-
-    def backward(i, _):
-        c = NC - 1 - i
+    unpack_state(ent2, u_ref.at[NC - 1])
+    for c in range(NC - 1, 0, -1):
+        u_ref[c - 1] = keep_ref[c] * u_ref[c] + r_ref[c]
+
+    def backward(c, _):
         rows = chunk_rows(c)
-        bc = bc_ref[rows, :]
-        b = bc[:, 0:N]
-        running = run_ref[rows, :]
-        last = running[L - 1:L, :]
-        grad = state_ref[...]
+        grad = u_ref[c]
         fade = fade_ref[rows, :]
         weighted = sc_ref[rows, :] * fade
-        d_weighted = wide_dot(b, grad)
-        used = dot_exact_right(d_weighted * weighted, cols)
+        d_weighted = wide_dot(bc_ref[rows, 0:N], grad)
+        used = dot((d_weighted * weighted).astype(BF16), cols)
         db = db_ref[rows, :] + three_dots(weighted, grad, NT)
-        keep = keep_row(last, heads)
-        held = jnp.sum(keep * grad * s_ref[c], axis=0, keepdims=True)
+        held = keep_ref[c] * jnp.sum(grad * s_ref[c], axis=0, keepdims=True)
         held = dot_exact_right(jnp.broadcast_to(held, (8, D)), cols)[0:1]
         d_scaled = d_weighted * fade + yin_ref[rows, :]
         d_running = q_ref[rows, :] - used
         d_last = jnp.sum(used, axis=0, keepdims=True) + held
         d_decay = dot_exact_left3(upper, d_running) + d_last
-        d_delta = dot_exact_right(d_scaled * v_ref[rows, :], cols) - rate * d_decay
-        gd = (d_delta * sigmoid(raw_ref[rows, :])).astype(BF16)
+        direct = dot((d_scaled * v_ref[rows, :]).astype(BF16), cols)
+        gd = ((direct - rate * d_decay) * sigmoid(raw_ref[rows, :])).astype(BF16)
         gd_ref[rows, :] = gd
         gp_ref[rows, 0:D] = (d_scaled * wid_ref[rows, :] + skip * dy_ref[rows, :]).astype(BF16)
         gp_ref[rows, D:PROJ] = jnp.concatenate([db, dc_ref[rows, :]], axis=1).astype(BF16)
-        state_ref[...] = r_ref[c] + keep * grad
-        gs = dot(gp_ref[rows, :], wp[...], NT) + dot(gd, wd[...])
+        gs = dot(gp_ref[rows, :], wpt[...]) + dot(gd, wd[...])
         tok[pl.ds(c * (L // BLK), L // BLK)] = gs.astype(BF16).reshape(L // BLK, BLK, D)
         return 0
 
-    lax.fori_loop(0, NC, backward, 0)
-
-    def send_back(d, _):
-        ret[d] = tok[idst_ref[0, d]]
-        return 0
-
-    lax.fori_loop(0, NSEQ, send_back, 0)
-    grads_back = Exchange(ret, back, lv_sems)
-    grads_back.start()
-    back[me] = ret[me]
-    deep2.spread()
-
+    lax.fori_loop(0, NC, backward, 0, unroll=UNROLL)
     gp = gp_ref[...]
     gd = gd_ref[...]
     for m in range(8):
-        xt = x_ref[:, 128 * m:128 * m + 128].T
+        xt = xt_ref[128 * m:128 * m + 128, :]
         rows_p = dot(xt, gp)
         rows_d = dot(xt, gd)
         dt_hi, dt_lo = split2(rows_d)
@@ -645,33 +656,53 @@
             pb[core, y, x, :, PROJ - HALF:HALF] = rows_d[sub]
     sum_a.start_pair()
     sum_b.start_pair()
+
+    def send_back(d, _):
+        ret[d] = tok[inv_ref[0, d]]
+        return 0
+
+    lax.fori_loop(0, NSEQ, send_back, 0, unroll=4)
+    grads_back = Exchange(ret, back, lv_sems)
+    grads_back.start(1, SPLIT)
+    back[me] = ret[me]
     sum_a.start_first()
     sum_b.start_first()
+    grads_back.start(SPLIT, NSEQ)
+    for k, plane in enumerate((sum_v, sum_w)):
+        sum_rows = plane.finish()
+        for i in range(4):
+            zs2[4 * k + i] = sum_rows[8 * i:8 * i + 8]
+    deep2.start()
     sum_a.start_second()
     sum_b.start_second()
+    deep2.spread()
     for k, plane in enumerate((sum_a, sum_b)):
         sum_rows = plane.finish()
         for i in range(4):
             zs1[4 * k + i] = sum_rows[8 * i:8 * i + 8]
     deep1.start()
+    deep2.finish()
+    deep1.spread()
     grads_back.wait()
-
-    def settle_back(j, _):
-        out_ref[j] = back[isrc_ref[0, j]]
-        return 0
-
-    lax.fori_loop(0, NSEQ, settle_back, 0)
-    deep2.finish()
-    for i in range(4):
-        for k in range(2):
-            go_out[8 * i:8 * i + 8, 512 * k:512 * k + 512] = zo2[4 * k + i]
-    deep1.spread()
     deep1.finish()
+
+
+def place_kernel(src_ref, back_ref, zo1_ref, zo2_ref, out_ref, gp_ref, gd_ref, go_ref):
+    def settle(j, _):
+        out_ref[src_ref[0, j]] = back_ref[j]
+        return 0
+
+    lax.fori_loop(0, NSEQ, settle, 0, unroll=4)
+    tails = []
     for i in range(4):
         rows = slice(8 * i, 8 * i + 8)
-        gp_out[rows, 0:HALF] = zo1[i]
-        gp_out[rows, HALF:PROJ] = zo1[4 + i, :, 0:PROJ - HALF]
-        gd_out[rows, :] = zo1[4 + i, :, PROJ - HALF:HALF]
+        for k in range(2):
+            go_ref[rows, 512 * k:512 * k + 512] = zo2_ref[4 * k + i]
+        gp_ref[rows, 0:HALF] = zo1_ref[i]
+        gp_ref[rows, HALF:PROJ] = zo1_ref[4 + i, :, 0:PROJ - HALF]
+        tails.append(zo1_ref[4 + i, :, PROJ - HALF:HALF])
+    turned = jnp.concatenate(tails, axis=0).T
+    gd_ref[...] = turned[0:H] + turned[H:2 * H]
 
 
 def local(tokens, grad_out, src_order, dst_order, w_proj, w_dt, w_out,
@@ -683,7 +714,7 @@
     full = vm((T, D), F32)
     low = vm((T, D), BF16)
     states = vm((NC, N, D), F32)
-    pay, piece = vm((NSEQ, 16, 256), F32), vm((NSEQ, 8, 256), F32)
+    pay, piece = vm((NSEQ, 8, 384), F32), vm((NSEQ, 8, 256), F32)
 
     def plane(width):
         line = vm((4, 32, width), BF16)
@@ -691,49 +722,55 @@
         return [vm((2, 4, 4, 32, width), BF16), square, square, square, line, line]
 
     scratch = (
-        [block, block, vm((D, PROJ), BF16), vm((H, D), BF16), vm((D, D), BF16)]
+        [block, block, vm((D, PROJ), BF16), vm((H, D), BF16), vm((D, D), BF16),
+         vm((PROJ, D), BF16), vm((D, D), BF16), vm((D, T), BF16)]
         + [block] * 4 + [low] * 2
         + [full, vm((T, 2 * N), F32), vm((T, H), F32), vm((T, H), F32), vm((NC, H, L), F32)]
         + [states] + [full] * 3
-        + [pay, pay, piece, piece] * 2
+        + [pay, pay] + [piece] * 6
         + [full, full, full, low, vm((T, H), F32), vm((T, N), F32), vm((T, N), F32)]
         + [states, states]
-        + [vm((N, D), F32), vm((T, PROJ), BF16), vm((T, H), BF16), block, block]
-        + plane(HALF) + plane(HALF) + plane(D)
-        + [vm((NDP, 8, HALF), F32)] * 3 + [vm((NDP, 8, 512), F32)] * 3
-        + [dma((5,))] + [dma((2,))] * 7 + [dma((6,))] * 3 + [dma((4,))] * 2
+        + [vm((N, D), F32), vm((NC, 1, D), F32), vm((T, PROJ), BF16), vm((T, H), BF16), block]
+        + [pltpu.SMEM((1, NSEQ), jnp.int32)]
+        + plane(HALF) + plane(HALF) + plane(512) + plane(512)
+        + [vm((NDP, 8, HALF), F32)] * 2 + [vm((NDP, 8, 512), F32)] * 2
+        + [dma((5,))] + [dma((2,))] * 7 + [dma((6,))] * 4 + [dma((4,))] * 2
     )
-    order = jnp.arange(NSEQ, dtype=jnp.int32)
-
-    def inverse(perm):
-        return jnp.sum(
-            jnp.where(perm[0][None, :] == order[:, None], order[None, :], 0), axis=1,
-            dtype=jnp.int32,
-        ).reshape(1, NSEQ)
-
     hbm = pl.BlockSpec(memory_space=pl.ANY)
-    grad_tokens, gp, gd, go = pl.pallas_call(
+    back, zo1, zo2 = pl.pallas_call(
         whole_kernel,
         out_shape=[
             jax.ShapeDtypeStruct(blocks, BF16),
-            jax.ShapeDtypeStruct((32, PROJ), F32),
-            jax.ShapeDtypeStruct((32, 128), F32),
-            jax.ShapeDtypeStruct((32, D), F32),
+            jax.ShapeDtypeStruct((NDP, 8, HALF), F32),
+            jax.ShapeDtypeStruct((NDP, 8, 512), F32),
         ],
-        in_specs=[SM] * 4 + [hbm] * 5 + [VM] * 4,
-        out_specs=[VM] * 4,
+        in_specs=[SM] * 2 + [hbm] * 5 + [VM] * 4,
+        out_specs=[VM] * 3,
         scratch_shapes=scratch,
         compiler_params=pltpu.CompilerParams(
             collective_id=0, has_side_effects=True, vmem_limit_bytes=VMEM_LIMIT
         ),
         name="whole",
     )(
-        src_order, dst_order, inverse(src_order), inverse(dst_order),
+        src_order, dst_order,
         tokens.reshape(blocks), grad_out.reshape(blocks), w_proj, w_dt.T, w_out,
         dt_bias.reshape(1, H), decay_rate.reshape(1, H), d_skip.reshape(1, H),
         norm_gain.reshape(1, D),
     )
-    return grad_tokens.reshape(1, T, D), gp, gd[:, 0:H] + gd[:, H:2 * H], go.T
+    grad_tokens, gp, gd, go = pl.pallas_call(
+        place_kernel,
+        out_shape=[
+            jax.ShapeDtypeStruct(blocks, BF16),
+            jax.ShapeDtypeStruct((32, PROJ), F32),
+            jax.ShapeDtypeStruct((H, 32), F32),
+            jax.ShapeDtypeStruct((32, D), F32),
+        ],
+        in_specs=[SM] + [VM] * 3,
+        out_specs=[VM] * 4,
+        compiler_params=pltpu.CompilerParams(vmem_limit_bytes=VMEM_LIMIT),
+        name="place",
+    )(src_order, back, zo1, zo2)
+    return grad_tokens.reshape(1, T, D), gp, gd.T, go.T
 
 
 def solution(mesh):

time: 147 us -> 127 us (0.86)
  Pallas kernels: 138 us -> 126 us
  local copies, waits for them, and re-layouts: 5.17 us -> 0 us
  other arithmetic: 3.43 us -> 0 us
    pallas_call x1, Pallas kernels: 138 us -> 124 us  [local(): pl.pallas_call(whole_kernel, out_shape=[jax.ShapeDtypeStruct(blocks, BF16...]
    unnamed x6 -> x0, local copies, waits for them, and re-layouts: 5.17 us -> none
    reduce_sum x2 -> x0, other arithmetic: 2.56 us -> none  [inverse(): jnp.sum(jnp.where(perm[0][None, :] == order[:, None], order[None, :], 0),...]
    pallas_call x0 -> x1, Pallas kernels: none -> 2.49 us  [local(): pl.pallas_call(place_kernel, out_shape=[jax.ShapeDtypeStruct(blocks, BF16...]
where the time goes in v3:
time: 127 us
  Pallas kernels  126 us (99%)
    pallas_call x1, Pallas kernels, local(): pl.pallas_call(whole_kernel, out_shape=[jax.ShapeDtypeStruct(blocks, BF16...  124 us

profile of v3, /device:TPU:24, one launch (start us, length us, event | category | flops | bytes accessed | tf_op | source)
XLA Modules:
  0.0 127.1 jit_solution(4903065677625904)
XLA Ops:
  0.6 124.0 %whole.1 = (bf16[32,16,1024]{2,1,0:T(8,128)(2,1)}, f32[8,8,640]{2,1,0:T(8,128)}, f32[8,8,512]{2,1,0:T(8,128)}) custom-call(s32[1,32]{1,0:T(1,128)} %src_ref.3, s32[1,32]{1,0:T(1,128)} %dst_ref.1, bf16[32,16,1024]{2,1,0:T(8,128)(2,1)} %bitcast.10, bf16[32,16,1024]{2,1,0:T(8,128)(2,1)} %bitcast.11, bf16[1024,1152]{1,0:T(8,128)(2,1)} %wp_hbm.1, ...), custom_call_target="tpu_custom_call" | custom-call | tf_op jit(solution)/shard_map/whole/pallas_call | solution.py:740
  124.6 2.5 %place.1 = (bf16[32,16,1024]{2,1,0:T(8,128)(2,1)}, f32[32,1152]{1,0:T(8,128)}, f32[16,32]{1,0:T(8,128)}, f32[32,1024]{1,0:T(8,128)}) custom-call(s32[1,32]{1,0:T(1,128)} %src_ref.3, bf16[32,16,1024]{2,1,0:T(8,128)(2,1)} %get-tuple-element.11.back_ref, f32[8,8,640]{2,1,0:T(8,128)} %get-tuple-element.12.zo1_ref, f32[8,8,512]{2,1,0:T(8,128)} %get-tuple-element.13.zo2_ref), custom_call_target="tpu_custom_call" | custom-call | tf_op jit(solution)/shard_map/place/pallas_call | solution.py:760

commit v4 on v3

--- a/solution.py
+++ b/solution.py
@@ -24,8 +24,9 @@
 MESH = pl.DeviceIdType.MESH
 VMEM_LIMIT = 62 * 1024 * 1024
 HALF = 640
-SPLIT = 13
+SPLIT = 32
 UNROLL = 2
+LATER = 1
 
 VM = pl.BlockSpec(memory_space=pltpu.VMEM)
 SM = pl.BlockSpec(memory_space=pltpu.SMEM)
@@ -344,12 +345,12 @@
 def whole_kernel(
     src_ref, dst_ref, tok_hbm, grad_hbm, wp_hbm, wd_hbm, wo_hbm,
     bias_ref, rate_ref, skip_ref, gain_ref,
-    back, zo1, zo2,
+    back_hbm, zo1, zo2,
     tok, grd, wp, wd, wo, wpt, wot, xt_ref, send_t, send_g, recv_t, recv_g, x_ref, g_ref,
     v_ref, bc_ref, raw_ref, run_ref, runt_ref, u_ref, sc_ref, wid_ref, fade_ref,
     pay1, got1, mid1, ent1, pay2, got2, mid2, ent2,
     yin_ref, gn_ref, dy_ref, low_ref, q_ref, dc_ref, db_ref, s_ref, r_ref,
-    state_ref, keep_ref, gp_ref, gd_ref, ret, inv_ref,
+    state_ref, keep_ref, gp_ref, gd_ref, ret, back, inv_ref,
     pa, ra_a, ta, rb_a, ha, rc_a, pb, ra_b, tb, rb_b, hb, rc_b,
     pv, ra_v, tv, rb_v, hv, rc_v, pw, ra_w, tw, rb_w, hw, rc_w,
     zs1, zr1, zs2, zr2,
@@ -641,20 +642,22 @@
         return 0
 
     lax.fori_loop(0, NC, backward, 0, unroll=UNROLL)
-    gp = gp_ref[...]
+    gp = gp_ref[:, 0:HALF]
+    for m in range(8):
+        rows_p = dot(xt_ref[128 * m:128 * m + 128, :], gp).astype(BF16)
+        for y, x, core, sub in spots(m):
+            pa[core, x, y] = rows_p[sub]
+    sum_a.start_pair()
+    gp = gp_ref[:, HALF:PROJ]
     gd = gd_ref[...]
     for m in range(8):
         xt = xt_ref[128 * m:128 * m + 128, :]
-        rows_p = dot(xt, gp)
-        rows_d = dot(xt, gd)
-        dt_hi, dt_lo = split2(rows_d)
-        rows_p = rows_p.astype(BF16)
+        rows_p = dot(xt, gp).astype(BF16)
+        dt_hi, dt_lo = split2(dot(xt, gd))
         rows_d = jnp.concatenate([dt_hi, dt_lo, jnp.zeros((128, 128 - 2 * H), BF16)], axis=1)
         for y, x, core, sub in spots(m):
-            pa[core, x, y] = rows_p[sub, 0:HALF]
-            pb[core, y, x, :, 0:PROJ - HALF] = rows_p[sub, HALF:PROJ]
+            pb[core, y, x, :, 0:PROJ - HALF] = rows_p[sub]
             pb[core, y, x, :, PROJ - HALF:HALF] = rows_d[sub]
-    sum_a.start_pair()
     sum_b.start_pair()
 
     def send_back(d, _):
@@ -663,11 +666,10 @@
 
     lax.fori_loop(0, NSEQ, send_back, 0, unroll=4)
     grads_back = Exchange(ret, back, lv_sems)
-    grads_back.start(1, SPLIT)
+    grads_back.start(1, LATER)
     back[me] = ret[me]
     sum_a.start_first()
     sum_b.start_first()
-    grads_back.start(SPLIT, NSEQ)
     for k, plane in enumerate((sum_v, sum_w)):
         sum_rows = plane.finish()
         for i in range(4):
@@ -675,6 +677,7 @@
     deep2.start()
     sum_a.start_second()
     sum_b.start_second()
+    grads_back.start(LATER, NSEQ)
     deep2.spread()
     for k, plane in enumerate((sum_a, sum_b)):
         sum_rows = plane.finish()
@@ -684,7 +687,10 @@
     deep2.finish()
     deep1.spread()
     grads_back.wait()
+    keep_back = pltpu.make_async_copy(back, back_hbm, load_sems.at[5])
+    keep_back.start()
     deep1.finish()
+    keep_back.wait()
 
 
 def place_kernel(src_ref, back_ref, zo1_ref, zo2_ref, out_ref, gp_ref, gd_ref, go_ref):
@@ -730,11 +736,11 @@
         + [pay, pay] + [piece] * 6
         + [full, full, full, low, vm((T, H), F32), vm((T, N), F32), vm((T, N), F32)]
         + [states, states]
-        + [vm((N, D), F32), vm((NC, 1, D), F32), vm((T, PROJ), BF16), vm((T, H), BF16), block]
+        + [vm((N, D), F32), vm((NC, 1, D), F32), vm((T, PROJ), BF16), vm((T, H), BF16), block, block]
         + [pltpu.SMEM((1, NSEQ), jnp.int32)]
         + plane(HALF) + plane(HALF) + plane(512) + plane(512)
         + [vm((NDP, 8, HALF), F32)] * 2 + [vm((NDP, 8, 512), F32)] * 2
-        + [dma((5,))] + [dma((2,))] * 7 + [dma((6,))] * 4 + [dma((4,))] * 2
+        + [dma((6,))] + [dma((2,))] * 7 + [dma((6,))] * 4 + [dma((4,))] * 2
     )
     hbm = pl.BlockSpec(memory_space=pl.ANY)
     back, zo1, zo2 = pl.pallas_call(
@@ -745,7 +751,7 @@
             jax.ShapeDtypeStruct((NDP, 8, 512), F32),
         ],
         in_specs=[SM] * 2 + [hbm] * 5 + [VM] * 4,
-        out_specs=[VM] * 3,
+        out_specs=[hbm, VM, VM],
         scratch_shapes=scratch,
         compiler_params=pltpu.CompilerParams(
             collective_id=0, has_side_effects=True, vmem_limit_bytes=VMEM_LIMIT

time: 127 us -> 116 us (0.913)
  the two profiles are of different devices: /device:TPU:24 before, /device:TPU:1 now
where the time goes in v4:
time: 116 us; the launch traced here: 115 us
  Pallas kernels  115 us (99%)
    pallas_call x1, Pallas kernels, local(): pl.pallas_call(whole_kernel, out_shape=[jax.ShapeDtypeStruct(blocks, BF16...  112 us
    pallas_call x1, Pallas kernels, local(): pl.pallas_call(place_kernel, out_shape=[jax.ShapeDtypeStruct(blocks, BF16...  2.49 us

profile of v4, /device:TPU:1, one launch (start us, length us, event | category | flops | bytes accessed | tf_op | source)
XLA Modules:
  0.0 115.4 jit_solution(16376935375736832545)
XLA Ops:
  0.6 112.3 %whole.1 = (bf16[32,16,1024]{2,1,0:T(8,128)(2,1)}, f32[8,8,640]{2,1,0:T(8,128)}, f32[8,8,512]{2,1,0:T(8,128)}) custom-call(s32[1,32]{1,0:T(1,128)} %src_ref.3, s32[1,32]{1,0:T(1,128)} %dst_ref.1, bf16[32,16,1024]{2,1,0:T(8,128)(2,1)} %bitcast.10, bf16[32,16,1024]{2,1,0:T(8,128)(2,1)} %bitcast.11, bf16[1024,1152]{1,0:T(8,128)(2,1)} %wp_hbm.1, ...), custom_call_target="tpu_custom_call" | custom-call | tf_op jit(solution)/shard_map/whole/pallas_call | solution.py:746
  112.9 2.5 %place.1 = (bf16[32,16,1024]{2,1,0:T(8,128)(2,1)}, f32[32,1152]{1,0:T(8,128)}, f32[16,32]{1,0:T(8,128)}, f32[32,1024]{1,0:T(8,128)}) custom-call(s32[1,32]{1,0:T(1,128)} %src_ref.3, bf16[32,16,1024]{2,1,0:T(8,128)(2,1)} %get-tuple-element.11.back_ref, f32[8,8,640]{2,1,0:T(8,128)} %get-tuple-element.12.zo1_ref, f32[8,8,512]{2,1,0:T(8,128)} %get-tuple-element.13.zo2_ref), custom_call_target="tpu_custom_call" | custom-call | tf_op jit(solution)/shard_map/place/pallas_call | solution.py:766
